TPU v7x, 512 devices: a whole 4x8x8 slice. The times are simulated.
512 devices in a mesh: team: 64 (over z_hi, y, core), loop: 8 (over z_lo, x).
Axes of the slice: x: 4, y: 8, z: 8 (z_hi: 4, z_lo: 2; z = z_hi * 2 + z_lo), core: 2. Of those that a mesh axis runs over, the one named last changes fastest.
Arguments:
- src_pos: float32 [3, 262144], P(None, ('team', 'loop')), may hold values from -6 to 6
- src_vel: float32 [3, 262144], P(None, ('team', 'loop')), may hold values from -5 to 5
- src_mass: float32 [262144], P(('team', 'loop')), may hold values from 0.2 to 5
- old_accel: float32 [6, 8192], P(None, ('team', 'loop')), may hold values from -6 to 6
- active_index: int32 [8192], P(('team', 'loop')), may hold values from 0 to 511, as said below
- active_level: int32 [8192], P(('team', 'loop')), may hold values from 0 to 3
- tile_id: int32 [8192], P(('team', 'loop')), may hold values from 0 to 511
- tile_offset: int32 [2, 8192], P(None, ('team', 'loop')), may hold values from 16 to 112
Outputs:
- new_state: float32 [12, 8192], P(None, ('team', 'loop'))
- image: float32 [2, 512, 128, 128], P(None, ('team', 'loop'))
Inputs may be any that keep to these rules, and one draw needn't show every extreme that they name: `active_index`: the 16 entries of one device are distinct rows of that device's 512 source stars.
All inputs are finite; a program needn't handle non-finite values.
Results may differ from a plain program's by a relative error of at most 0.0027.
Values sent between devices are 32-bit elements; how exact they have to be, the bound alone decides.
A program may use at most 64 MiB of HBM per device.

v0:
```python
import math

import jax
import jax.numpy as jnp
from jax import lax
from jax.sharding import PartitionSpec as P

TILE_DEV = 1
TILE_W = 128


def from_behind(block, axis, distance):
    devices = range(lax.axis_size(axis))
    route = [((i - distance) % len(devices), i) for i in devices]
    return lax.ppermute(block, axis, route)


def pair_terms(tgt_pos, tgt_vel, blk_pos, blk_vel, blk_mass, gravity, soften_sq):
    separation = blk_pos[:, None, :] - tgt_pos[:, :, None]
    rel_vel = blk_vel[:, None, :] - tgt_vel[:, :, None]
    dist_sq = jnp.sum(separation * separation, axis=0) + soften_sq
    inverse = lax.rsqrt(dist_sq)
    inverse_sq = inverse * inverse
    strength = (gravity * blk_mass)[None, :] * inverse * inverse_sq
    radial = 3.0 * jnp.sum(separation * rel_vel, axis=0) * inverse_sq
    acceleration = jnp.sum(strength[None] * separation, axis=2)
    jerk_sum = jnp.sum(strength[None] * (rel_vel - radial[None] * separation), axis=2)
    return jnp.concatenate([acceleration, jerk_sum], axis=0)


def correct(targets, force, old_accel, level_float):
    step_len = jnp.exp2(-level_float)
    accel_gap = old_accel[0:3] - force[0:3]
    first_term = -6.0 * accel_gap - step_len * (4.0 * old_accel[3:6] + 2.0 * force[3:6])
    second = 12.0 * accel_gap + 6.0 * step_len * (old_accel[3:6] + force[3:6])
    new_pos = targets[0:3] + step_len * step_len * (first_term / 24.0 + second / 120.0)
    new_vel = targets[3:6] + step_len * (first_term / 6.0 + second / 24.0)
    return jnp.concatenate([new_pos, new_vel, force], axis=0)


def ingredients(new_state, star_mass, offsets, width):
    swing_cells = width / 16.0
    centre_y = offsets[0] + swing_cells * jnp.tanh(new_state[1])
    centre_x = offsets[1] + swing_cells * jnp.tanh(new_state[0])
    return jnp.stack([star_mass, star_mass * new_state[5] * new_state[5], centre_y, centre_x])


def kernel_rows(centre, width):
    cell_mid = jnp.arange(width, dtype=jnp.float32) + 0.5
    scaled = (cell_mid[None, :] - centre[:, None]) / (width / 40.0)
    return jnp.exp(-0.5 * scaled * scaled)


def block_forces(targets, source, gravity, soften_sq):
    source_len = source.shape[1]
    block_len = math.gcd(source_len, 512)
    blocks = source.reshape(7, source_len // block_len, block_len).transpose(1, 0, 2)

    def add_block(running, block_now):
        return (
            running
            + pair_terms(
                targets[0:3],
                targets[3:6],
                block_now[0:3],
                block_now[3:6],
                block_now[6],
                gravity,
                soften_sq,
            ),
            None,
        )

    return lax.scan(add_block, jnp.zeros((6, targets.shape[1]), jnp.float32), blocks)[0]


def shards(src_pos, src_vel, src_mass, old_accel, active_index, active_level, tile_id, tile_offset):
    total_stars = src_pos.shape[1] * lax.axis_size("team") * lax.axis_size("loop")
    gravity = 1.0 / total_stars
    soften_sq = float(total_stars) ** (-2.0 / 3.0)
    own_records = jnp.concatenate(
        [jnp.take(src_pos, active_index, axis=1), jnp.take(src_vel, active_index, axis=1)], axis=0
    )
    own_mass = jnp.take(src_mass, active_index, axis=0)
    source = jnp.concatenate([src_pos, src_vel, src_mass[None]], axis=0)
    owned_tiles = lax.axis_index(("team", "loop")) * TILE_DEV + jnp.arange(
        TILE_DEV, dtype=jnp.int32
    )
    empty_image = jnp.zeros((2, TILE_DEV, TILE_W, TILE_W), jnp.float32)
    targets = lax.all_gather(own_records, "team", axis=1, tiled=True)
    total_force = block_forces(targets, source, gravity, soften_sq)
    moving = source
    for turn in range(lax.axis_size("loop") - 1):
        moving = from_behind(moving, "loop", 1)
        total_force = total_force + block_forces(targets, moving, gravity, soften_sq)
    own_force = lax.psum_scatter(total_force, "team", scatter_dimension=1, tiled=True)
    new_state = correct(own_records, own_force, old_accel, active_level.astype(jnp.float32))
    deposit_parts = ingredients(new_state, own_mass, tile_offset.astype(jnp.float32), TILE_W)
    deposit_deposit_parts = lax.all_gather(deposit_parts, ("team", "loop"), axis=1, tiled=True)
    tile_rows = lax.all_gather(tile_id[None], ("team", "loop"), axis=1, tiled=True)
    row_count = deposit_deposit_parts.shape[1]
    star_block = math.gcd(row_count, 256)
    order = jnp.argsort(tile_rows[0], stable=True)
    sorted_tiles = jnp.take(tile_rows[0], order, axis=0)
    sorted_parts = jnp.take(deposit_deposit_parts, order, axis=1)
    low_row = jnp.sum((sorted_tiles < owned_tiles[0]).astype(jnp.int32))
    high_row = jnp.sum((sorted_tiles <= owned_tiles[TILE_DEV - 1]).astype(jnp.int32))
    first_block = low_row // star_block
    end_block = (high_row + star_block - 1) // star_block

    def add_stars(block_idx, running):
        first_row = block_idx * star_block
        part_block = lax.dynamic_slice_in_dim(sorted_parts, first_row, star_block, 1)
        tile_block = lax.dynamic_slice_in_dim(sorted_tiles, first_row, star_block, 0)
        tile_mask = (tile_block[None, :] == owned_tiles[:, None]).astype(jnp.float32)
        weighted = part_block[0:2, :, None] * kernel_rows(part_block[2], TILE_W)[None]
        left_rows = (weighted[:, None] * tile_mask[None, :, :, None]).astype(jnp.bfloat16)
        right_rows = kernel_rows(part_block[3], TILE_W).astype(jnp.bfloat16)
        return running + jnp.einsum(
            "ltsy,sx->ltyx", left_rows, right_rows, preferred_element_type=jnp.float32
        )

    image = lax.fori_loop(first_block, end_block, add_stars, empty_image)
    return (new_state, image)


def solution(mesh):
    return jax.shard_map(
        shards,
        mesh=mesh,
        in_specs=(
            P(None, ("team", "loop")),
            P(None, ("team", "loop")),
            P(("team", "loop")),
            P(None, ("team", "loop")),
            P(("team", "loop")),
            P(("team", "loop")),
            P(("team", "loop")),
            P(None, ("team", "loop")),
        ),
        out_specs=(P(None, ("team", "loop")), P(None, ("team", "loop"), None, None)),
        check_vma=False,
    )
```

profile of v0, /device:TPU:1, one launch (start us, length us, event | category | flops | bytes accessed | tf_op | source)
XLA Modules:
  0.0 1770.9 jit_solution(9198500476613658640)
XLA Ops:
  7.2 0.0 reduce-scatter.4.cloned.1.call-start
  7.2 0.7 pad_maximum_fusion
  8.0 3.9 collective-permute-start
  11.9 0.8 copy.89
  12.8 0.8 copy.91
  13.6 0.7 compare_select_fusion.1
  14.3 0.7 compare_and_fusion.1
  14.9 0.6 gather_fusion.3
  15.5 0.1 copy.90
  15.6 0.6 gather_fusion.4
  16.1 0.1 copy.92
  16.2 89.8 %all-gather.1 = f32[64,16,6]{1,2,0:T(8,128)S(1)} all-gather(f32[1,16,6]{1,2,0:T(8,128)S(1)} %maximum_bitcast_fusion), channel_id=1, replica_groups=mesh['team'=64,'loop'=8] {'team'}, dimensions={0}, use_global_device_ids=true | all-gather | bytes 24960 | tf_op jit(solution)/shard_map/all_gather | solution.py:90
  106.0 0.1 reshape.421
  106.2 0.9 dynamic-update-slice
  107.1 95.4 %all-reduce = s32[8192]{0:T(1024)S(1)} all-reduce(s32[8192]{0:T(1024)S(1)} %dynamic-update-slice), channel_id=2, replica_groups=mesh['team'=64,'loop'=8] {'team','loop'}, use_global_device_ids=true, to_apply=%add | all-reduce | flops 8192 | bytes 65536
  202.5 6.8 sort.17
  209.3 45.5 %gather_fusion = s32[8192]{0:T(1024)S(1)} fusion(s32[8192]{0:T(1024)S(1)} %all-reduce, s32[8192]{0:T(1024)S(1)} %fusion.63), kind=kCustom, calls=%fused_computation.2 | custom fusion | bytes 98304 | tf_op jit(solution)/shard_map/jit(_take)/gather | solution.py:104
  254.8 0.6 convert_reduce_fusion
  255.5 2.3 collective-permute-start.1
  257.8 4.3 collective-permute-done.1
  262.1 1.8 fusion.39
  263.9 1.9 collective-permute-start.2
  265.8 0.7 multiply_multiply_fusion.10
  266.5 3.9 collective-permute-done.2
  270.5 1.9 collective-permute-start.3
  272.4 4.6 collective-permute-done.3
  277.1 8.1 fusion.40
  285.2 1.6 multiply_multiply_fusion.7
  286.8 2.1 collective-permute-start.4
  288.9 2.6 multiply_multiply_fusion.14
  291.6 1.8 collective-permute-done.4
  293.4 1.9 collective-permute-start.5
  295.4 4.6 collective-permute-done.5
  300.0 1.9 collective-permute-start.6
  301.9 4.6 collective-permute-done.6
  306.6 14.1 fusion.37
  320.7 3.0 multiply_multiply_fusion.8
  323.6 3.0 fusion.43
  326.7 0.7 multiply_multiply_fusion.5
  327.3 0.7 multiply_multiply_fusion.3
  328.0 0.7 multiply_multiply_fusion.1
  328.7 0.9 copy-done.1
  329.6 0.6 copy-done.2
  330.3 10.1 fusion.34
  340.4 0.1 fusion.62
  340.5 1.0 copy.97
  341.5 0.0 reduce-scatter.4.cloned.1.call-update
  341.5 0.7 gather_fusion.1
  345.2 138.2 %reduce-scatter.4.cloned.1.call-done = f32[16,6]{1,0:T(8,128)} async-done(((f32[1024,6]{1,0:T(8,128)}), f32[16,6]{1,0:T(8,128)}) %reduce-scatter.4.cloned.1.call-update) | async-done | bytes 400
  483.4 0.8 copy.98
  484.2 0.6 pad_maximum_fusion.1
  484.9 1233.1 %all-gather.2 = f32[512,16,4]{1,2,0:T(4,128)S(1)} all-gather(f32[1,16,4]{1,2,0:T(4,128)S(1)} %maximum_bitcast_fusion.1), channel_id=1, replica_groups=mesh['team'=64,'loop'=8] {'team','loop'}, dimensions={0}, use_global_device_ids=true | all-gather | bytes 131328 | tf_op jit(solution)/shard_map/all_gather | solution.py:99
  1717.9 4.5 copy.94
  1722.4 29.9 %gather_fusion.2 = f32[8192,4]{1,0:T(8,128)} fusion(f32[4,8192]{0,1:T(8,128)} %bitcast.52, s32[8192]{0:T(1024)S(1)} %fusion.63), kind=kCustom, calls=%fused_computation.4 | custom fusion | bytes 294912 | tf_op jit(solution)/shard_map/jit(_take)/gather | solution.py:105
  1752.3 7.4 select_bitcast_fusion
  1759.8 2.8 copy.95
  1762.7 0.7 while.9
  1762.7 0.1 fusion.79
  1762.8 0.1 fusion.80
  1762.9 0.1 copy.100
  1763.0 0.1 compare_convert_fusion.2
  1763.1 0.3 fusion.81
  1763.4 0.0 copy-start.5
  1763.4 0.6 copy-done.5
  (50 shorter events, 0.3 us)
Async XLA Ops:
  7.2 476.2 %reduce-scatter.4.cloned.1.call-start = ((), (), s32[]{:S(2)}) async-start(), calls=%async_computation.1 | async-start | bytes 532480
  8.0 247.5 %collective-permute-start = (f32[7,512]{1,0:T(8,128)S(1)}, f32[7,512]{1,0:T(8,128)S(1)}, u32[]{:S(2)}, u32[]{:S(2)}) collective-permute-start(f32[7,512]{1,0:T(8,128)S(1)} %pad_maximum_fusion), channel_id=1, source_target_pairs={{7,0},{0,1},{1,2},{2,3},{3,4},{4,5},{5,6},{6,7},{15,8},{8,9},{9,10... | collective-permute-start | bytes 43016 | tf_op jit(solution)/shard_map/ppermute | solution.py:15
  209.3 46.2 %copy-start = (f32[512]{0:T(512)S(1)}, f32[512]{0:T(512)}, u32[]{:S(2)}) copy-start(f32[512]{0:T(512)} %param.14) | copy-start | bytes 6148
  255.5 6.6 collective-permute-start.1
  263.9 6.6 collective-permute-start.2
  265.8 11.3 copy-start.3
  265.8 11.2 copy-start.4
  270.5 6.6 collective-permute-start.3
  286.8 6.6 collective-permute-start.4
  293.4 6.6 collective-permute-start.5
  300.0 6.6 collective-permute-start.6
  328.0 1.6 copy-start.1
  328.0 2.2 copy-start.2
  330.2 11.3 copy-start.9
  330.2 14.9 copy-start.7
  330.2 153.9 %copy-start.6 = (f32[6,16]{1,0:T(8,128)S(1)}, f32[6,16]{1,0:T(8,128)}, u32[]{:S(2)}) copy-start(f32[6,16]{1,0:T(8,128)} %param.15) | copy-start | bytes 1156
  330.2 154.0 %copy-start.8 = (s32[16]{0:T(128)S(1)}, s32[16]{0:T(128)}, u32[]{:S(2)}) copy-start(s32[16]{0:T(128)} %param.16) | copy-start | bytes 196
  1763.4 0.7 copy-start.5
Sparse Core Ops, SparseCore 0:
  341.6 141.7 reduce-scatter.3
where the time goes:
time: 1790 us; the launch traced here: 1770 us
  blocking collectives  1420 us (79%)
  waiting for transfers between devices  162 us (9%)
  local copies, waits for them, and re-layouts  91.7 us (5%)
  other arithmetic  65 us (4%)
    all_gather x1, blocking collectives, shards(): lax.all_gather(deposit_parts, ('team', 'loop'), axis=1, tiled=True)  1230 us
    unnamed x2, waiting for transfers between devices  138 us
    unnamed x1, blocking collectives  95.4 us
    all_gather x1, blocking collectives, shards(): targets = lax.all_gather(own_records, 'team', axis=1, tiled=True)  89.8 us
    gather x1, local copies, waits for them, and re-layouts, shards(): sorted_tiles = jnp.take(tile_rows[0], order, axis=0)  45.5 us
  transfers between devices with their start and end apart: 8, of which 7 were waited for; matrix products, arithmetic and copies ran while one was open for 4% of the time, Pallas kernels for 0%

commit v1 on v0

v1 whole, which is shorter than its diff:
```python
import functools

import jax
import jax.numpy as jnp
from jax import lax
from jax.experimental import pallas as pl
from jax.experimental.pallas import tpu as pltpu
from jax.sharding import PartitionSpec as P

MESH = pl.DeviceIdType.MESH
F32, BF16 = jnp.float32, jnp.bfloat16
RING = 8
SRC = 512
ACT = 16
LANES = 128
TILE_W = 128
ROWS_B = 256


def split3(v):
    a = v.astype(BF16)
    r = v - a.astype(F32)
    b = r.astype(BF16)
    return a, b, (r - b.astype(F32)).astype(BF16)


def wide3(v):
    return [p.astype(F32) for p in split3(v)]


def wide2(v):
    a = v.astype(BF16).astype(F32)
    return a, (v - a).astype(BF16).astype(F32)


def coarse(v):
    return jnp.round(v * 32.0) * (1.0 / 32.0)


def pad_rows(v, rows):
    gap = jnp.zeros((rows - v.shape[0], v.shape[1]), v.dtype)
    return jnp.concatenate([v, gap], axis=0)


def features(pos, vel, soften):
    h, u = coarse(pos), coarse(vel)
    l, m = pos - h, vel - u
    l1, l2 = wide2(l)
    m1, m2 = wide2(m)
    total = lambda v: jnp.sum(v, axis=0, keepdims=True)
    hh = wide3(total(h * h))
    hl = wide3(total(2.0 * h * l + l * l) + (0.0 if soften is None else soften))
    hu = wide3(total(h * u))
    hm = wide3(total(h * m + l * u + l * m))
    ones = [jnp.ones_like(h)]
    if soften is None:
        near = [h] + hh + ones + [h, h, l1, l2, l1, l1, l2] + hl + ones
        dots = [h, u] + hu + ones + [h, h, m1, m2, l1, l2, u, u, l1, l1, l2, m1, m1, m2] + hm + ones
    else:
        near = [-2.0 * h] + ones + hh
        near += [-2.0 * l1, -2.0 * l2, -2.0 * h, -2.0 * h, -2.0 * l1, -2.0 * l2, -2.0 * l1] + ones + hl
        dots = [-u, -h] + ones + hu
        dots += [-m1, -m2, -h, -h, -u, -u, -l1, -l2, -m1, -m2, -m1, -l1, -l2, -l1] + ones + hm
    near = jnp.concatenate(near, axis=0)
    return near.shape[0], pad_rows(jnp.concatenate([near] + dots, axis=0), LANES)


def correct(targets, force, old_accel, level):
    step = jnp.exp2(-level)
    gap = old_accel[0:3] - force[0:3]
    first = -6.0 * gap - step * (4.0 * old_accel[3:6] + 2.0 * force[3:6])
    second = 12.0 * gap + 6.0 * step * (old_accel[3:6] + force[3:6])
    pos = targets[0:3] + step * step * (first / 24.0 + second / 120.0)
    vel = targets[3:6] + step * (first / 6.0 + second / 24.0)
    return jnp.concatenate([pos, vel, force], axis=0)


def kernel(
    gravity, soften,
    pos_ref, vel_ref, mass_ref, old_ref, index_ref, level_ref, tile_ref, offset_ref,
    state_ref, image_ref,
    source, small, own, own_in, block, targets, near_f, dots_f, weights, target_f, force_acc,
    part, part_in, half, half_in, spread, gathered, left, right,
    send_sem, recv_sem,
):
    team, loop = lax.axis_index("team"), lax.axis_index("loop")
    zh, y, c = team // 16, (team // 2) % 8, team % 2
    zl, x = loop // 4, loop % 4
    z, xc = zh * 2 + zl, x * 2 + c

    def at(y, z, xc):
        return ((z // 2) * 16 + y * 2 + xc % 2, (z % 2) * 4 + xc // 2)

    def y_peer(k):
        return at((y + k) % 8, z, xc)

    def z_peer(k):
        return at(y, (z + k) % 8, xc)

    def x_peer(k):
        return at(y, z, (xc + k) % 8)

    barrier = pltpu.get_barrier_semaphore()
    for k in range(1, RING):
        for peer in (y_peer(k), z_peer(k), x_peer(k)):
            pl.semaphore_signal(barrier, inc=1, device_id=peer, device_id_type=MESH)

    def copy(stage, k, src, dst, peer):
        return pltpu.make_async_remote_copy(
            src_ref=src,
            dst_ref=dst,
            send_sem=send_sem.at[stage, k],
            recv_sem=recv_sem.at[stage, k],
            device_id=peer,
            device_id_type=MESH,
        )

    source[0, 0:3, :] = pos_ref[...]
    source[0, 3:6, :] = vel_ref[...]
    source[0, 6:7, :] = mass_ref[...].reshape(1, SRC)
    source[0, 7:8, :] = jnp.zeros((1, SRC), F32)
    small[...] = jnp.zeros_like(small)
    small[0:6, 0:ACT] = old_ref[...]
    small[6:7, 0:ACT] = level_ref[...].reshape(1, ACT).astype(F32)
    small[7:8, 0:ACT] = tile_ref[...].reshape(1, ACT).astype(F32)
    small[8:10, 0:ACT] = offset_ref[...].astype(F32)
    small[10:11, 0:ACT] = index_ref[...].reshape(1, ACT).astype(F32)
    placed = pltpu.roll(small[...], y * ACT, 1)
    star = lax.broadcasted_iota(jnp.int32, (SRC, LANES), 0).astype(F32)
    lane = lax.broadcasted_iota(jnp.int32, (SRC, LANES), 1)
    chosen = jnp.where((star == placed[10:11]) & (lane // ACT == y), 1.0, 0.0).astype(BF16)
    pieces = jnp.concatenate(wide3(source[0]), axis=0).astype(BF16)
    picked = jnp.dot(pieces, chosen, preferred_element_type=F32)
    own[0:8, :] = picked[0:8] + picked[8:16] + picked[16:24]
    own[8:24, :] = placed

    pl.semaphore_wait(barrier, 3 * (RING - 1))

    to_y = [copy(0, k, own, own_in.at[k], y_peer(k)) for k in range(1, RING)]
    to_z = [copy(1, k, source.at[0], source.at[k], z_peer(k)) for k in range(1, RING)]
    for k in range(1, RING):
        to_y[k - 1].start()
    for k in range(1, RING):
        to_z[k - 1].start()

    def prepare_source(k):
        s = source[k]
        cut, f = features(s[0:3], s[3:6], None)
        row = lax.broadcasted_iota(jnp.int32, f.shape, 0)
        lanes = pl.ds(pl.multiple_of(k * SRC, SRC), SRC)
        near_f[:, lanes] = jnp.where(row < cut, f, 0.0).astype(BF16)
        dots_f[:, lanes] = jnp.where(row < cut, 0.0, f).astype(BF16)
        mass = s[6:7]
        moments = jnp.concatenate([s[0:3] * mass, s[3:6] * mass, mass, jnp.zeros_like(mass)], axis=0)
        moments = pad_rows(jnp.concatenate(wide3(moments), axis=0), LANES)
        columns = jnp.transpose(moments)
        weights[0, lanes, :] = columns.astype(BF16)
        weights[1, lanes, :] = pltpu.roll(columns, 32, 1).astype(BF16)

    prepare_source(0)

    full = own[...]
    for k in range(1, RING):
        to_y[k - 1].wait_recv()
        full = full + own_in[k]
    block[...] = full[8:24]
    targets[0] = full[0:8]

    to_x = [copy(2, k, targets.at[0], targets.at[k], x_peer(k)) for k in range(1, RING)]
    for k in range(1, RING):
        to_x[k - 1].start()

    for k in range(1, RING):
        to_z[k - 1].wait_recv()

    def prepare_step(k, carry):
        prepare_source(k)
        return carry

    lax.fori_loop(1, RING, prepare_step, 0)

    for k in range(1, RING):
        to_x[k - 1].wait_recv()

    def prepare_target(k, carry):
        t = targets[k]
        f = features(t[0:3], t[3:6], soften)[1]
        target_f[pl.ds(pl.multiple_of(k * LANES, LANES), LANES), :] = jnp.transpose(f).astype(BF16)
        return carry

    lax.fori_loop(0, RING, prepare_target, 0)

    def force_step(step, carry):
        rows = pl.ds(pl.multiple_of(step * ROWS_B, ROWS_B), ROWS_B)
        f = target_f[rows, :]
        dist_sq = jnp.dot(f, near_f[...], preferred_element_type=F32)
        dots = jnp.dot(f, dots_f[...], preferred_element_type=F32)
        inverse = lax.rsqrt(dist_sq)
        inverse_sq = inverse * inverse
        strength = inverse * inverse_sq
        radial = (strength * inverse_sq) * dots
        force_acc[rows, :] = jnp.dot(
            strength.astype(BF16), weights[0], preferred_element_type=F32
        ) + jnp.dot(radial.astype(BF16), weights[1], preferred_element_type=F32)
        return carry

    lax.fori_loop(0, RING * LANES // ROWS_B, force_step, 0)

    def combine_step(k, carry):
        sums = jnp.transpose(force_acc[pl.ds(pl.multiple_of(k * LANES, LANES), LANES), :])
        plain = sums[0:8] + sums[8:16] + sums[16:24]
        tilted = sums[32:40] + sums[40:48] + sums[48:56]
        t = targets[k]
        accel = plain[0:3] - t[0:3] * plain[6:7]
        jerk = (plain[3:6] - t[3:6] * plain[6:7]) - 3.0 * (tilted[0:3] - t[0:3] * tilted[6:7])
        part[k] = pad_rows(gravity * jnp.concatenate([accel, jerk], axis=0), 8)
        return carry

    lax.fori_loop(0, RING, combine_step, 0)

    back_x = [copy(3, k, part.at[k], part_in.at[k], x_peer(-k)) for k in range(1, RING)]
    for k in range(1, RING):
        back_x[k - 1].start()
    total = part[0]
    for k in range(1, RING):
        back_x[k - 1].wait_recv()
        total = total + part_in[k]
    half[...] = total
    around_y = [copy(4, k, half, half_in.at[k], y_peer(k)) for k in range(1, RING)]
    for k in range(1, RING):
        around_y[k - 1].start()
    for k in range(1, RING):
        around_y[k - 1].wait_recv()
        total = total + half_in[k]

    stars = targets[0]
    rest = block[...]
    state = correct(stars[0:6], total[0:6], rest[0:6], rest[6:7])
    centre_y = rest[8:9] + (TILE_W / 16.0) * jnp.tanh(state[1:2])
    centre_x = rest[9:10] + (TILE_W / 16.0) * jnp.tanh(state[0:1])
    mass = stars[6:7]
    spread[0] = pad_rows(
        jnp.concatenate([mass, mass * state[5:6] * state[5:6], centre_y, centre_x, rest[7:8]], axis=0), 8
    )
    deposit_z = [copy(5, k, spread.at[0], spread.at[k], z_peer(k)) for k in range(1, RING)]
    for k in range(1, RING):
        deposit_z[k - 1].start()
    shifted = pltpu.roll(pad_rows(state, 16), (LANES - y * ACT) % LANES, 1)
    state_ref[...] = shifted[0:12, 0:ACT]
    for k in range(1, RING):
        deposit_z[k - 1].wait_recv()
    deposit_x = [copy(6, k, spread, gathered.at[k], x_peer(k)) for k in range(1, RING)]
    for k in range(1, RING):
        deposit_x[k - 1].start()

    mine = (team * 8 + loop).astype(F32)
    cell = lax.broadcasted_iota(jnp.int32, (TILE_W, LANES), 0).astype(F32) + 0.5

    def kernel_of(centre):
        scaled = (cell - centre) * (40.0 / TILE_W)
        return jnp.exp(-0.5 * (scaled * scaled))

    def add_stars(blocks, first):
        for b in range(RING):
            rows = blocks(b)
            here = rows[4:5] == mine
            rows_y, rows_x = kernel_of(rows[2:3]), kernel_of(rows[3:4])
            lanes = slice(b * LANES, (b + 1) * LANES)
            left[0:TILE_W, lanes] = (jnp.where(here, rows[0:1], 0.0) * rows_y).astype(BF16)
            left[TILE_W:, lanes] = (jnp.where(here, rows[1:2], 0.0) * rows_y).astype(BF16)
            right[:, lanes] = rows_x.astype(BF16)
        out = lax.dot_general(left[...], right[...], (((1,), (1,)), ((), ())), preferred_element_type=F32)
        out = out.reshape(2, 1, TILE_W, TILE_W)
        if first:
            image_ref[...] = out
        else:
            image_ref[...] += out

    add_stars(lambda b: spread[b], True)
    for k in range(1, RING):
        deposit_x[k - 1].wait_recv()

    def deposit_step(k, carry):
        add_stars(lambda b: gathered[k, b], False)
        return carry

    lax.fori_loop(1, RING, deposit_step, 0)
    for sent in (to_y, to_z, to_x, back_x, around_y, deposit_z, deposit_x):
        for one in sent:
            one.wait_send()


def shards(*arrays):
    stars = SRC * RING**3
    stage_count = 7
    vmem = pl.BlockSpec(memory_space=pltpu.VMEM)
    return pl.pallas_call(
        functools.partial(kernel, 1.0 / stars, float(stars) ** (-2.0 / 3.0)),
        out_shape=(
            jax.ShapeDtypeStruct((12, ACT), F32),
            jax.ShapeDtypeStruct((2, 1, TILE_W, TILE_W), F32),
        ),
        in_specs=[vmem] * len(arrays),
        out_specs=(vmem, vmem),
        scratch_shapes=[
            pltpu.VMEM((RING, 8, SRC), F32),
            pltpu.VMEM((16, LANES), F32),
            pltpu.VMEM((24, LANES), F32),
            pltpu.VMEM((RING, 24, LANES), F32),
            pltpu.VMEM((16, LANES), F32),
            pltpu.VMEM((RING, 8, LANES), F32),
            pltpu.VMEM((LANES, RING * SRC), BF16),
            pltpu.VMEM((LANES, RING * SRC), BF16),
            pltpu.VMEM((2, RING * SRC, LANES), BF16),
            pltpu.VMEM((RING * LANES, LANES), BF16),
            pltpu.VMEM((RING * LANES, LANES), F32),
            pltpu.VMEM((RING, 8, LANES), F32),
            pltpu.VMEM((RING, 8, LANES), F32),
            pltpu.VMEM((8, LANES), F32),
            pltpu.VMEM((RING, 8, LANES), F32),
            pltpu.VMEM((RING, 8, LANES), F32),
            pltpu.VMEM((RING, RING, 8, LANES), F32),
            pltpu.VMEM((2 * TILE_W, RING * LANES), BF16),
            pltpu.VMEM((TILE_W, RING * LANES), BF16),
            pltpu.SemaphoreType.DMA((stage_count, RING)),
            pltpu.SemaphoreType.DMA((stage_count, RING)),
        ],
        compiler_params=pltpu.CompilerParams(
            collective_id=0, has_side_effects=True, vmem_limit_bytes=48 << 20
        ),
        name="cluster_step",
    )(*arrays)


def solution(mesh):
    both = ("team", "loop")
    columns, rows = P(None, both), P(both)
    return jax.shard_map(
        shards,
        mesh=mesh,
        in_specs=(columns, columns, rows, columns, rows, rows, rows, columns),
        out_specs=(columns, P(None, both, None, None)),
        check_vma=False,
    )
```

time: 1790 us -> 66.4 us (0.04); the launches traced: 1770 us -> 66.1 us
  blocking collectives: 1420 us -> 0 us
  waiting for transfers between devices: 162 us -> 0 us
  local copies, waits for them, and re-layouts: 91.7 us -> 6.65 us
  other arithmetic: 65 us -> 0 us
  Pallas kernels: 0 us -> 58.8 us
    all_gather x2 -> x0, blocking collectives: 1320 us -> none  [the longest x1 1230 us: shards(): lax.all_gather(deposit_parts, ('team', 'loop'), axis=1, tiled=True)]
    unnamed x2 -> x0, waiting for transfers between devices: 138 us -> none
    unnamed x1 -> x0, blocking collectives: 95.4 us -> none
    gather x7 -> x0, local copies, waits for them, and re-layouts: 77.4 us -> none  [the longest x1 45.5 us: shards(): sorted_tiles = jnp.take(tile_rows[0], order, axis=0)]
    pallas_call x0 -> x1, Pallas kernels: none -> 58.8 us  [shards(): pl.pallas_call(functools.partial(kernel, 1.0 / stars, float(stars) ** (-2...]
    reduce_sum x6 -> x0, other arithmetic: 37.8 us -> none  [the longest x4 35.4 us: pair_terms(): acceleration = jnp.sum(strength[None] * separation, axis=2)]
    ppermute x7 -> x0, waiting for transfers between devices: 24 us -> none  [from_behind(): return lax.ppermute(block, axis, route)]
  transfers between devices with their start and end apart: 8 -> 0, of which waited for: 7 -> 0; matrix products, arithmetic and copies ran while one was open for 4% -> 0% of each run, Pallas kernels for 0% -> 0%
where the time goes in v1:
time: 66.4 us; the launch traced here: 66.1 us
  Pallas kernels  58.8 us (89%)
  local copies, waits for them, and re-layouts  6.65 us (10%)
    pallas_call x1, Pallas kernels, shards(): pl.pallas_call(functools.partial(kernel, 1.0 / stars, float(stars) ** (-2...  58.8 us
    unnamed x18, local copies, waits for them, and re-layouts  6.65 us

profile of v1, /device:TPU:1, one launch (start us, length us, event | category | flops | bytes accessed | tf_op | source)
XLA Modules:
  0.0 66.1 jit_solution(15957257304634408264)
XLA Ops:
  0.6 0.0 copy-start
  0.6 0.7 %copy-done = f32[3,512]{1,0:T(4,128)S(1)} copy-done((f32[3,512]{1,0:T(4,128)S(1)}, f32[3,512]{1,0:T(4,128)}, u32[]{:S(2)}) %copy-start) | copy-done | bytes 6168
  1.3 0.0 copy-start.1
  1.3 0.7 %copy-done.1 = f32[3,512]{1,0:T(4,128)S(1)} copy-done((f32[3,512]{1,0:T(4,128)S(1)}, f32[3,512]{1,0:T(4,128)}, u32[]{:S(2)}) %copy-start.1) | copy-done | bytes 6168
  2.0 0.0 copy-start.2
  2.0 0.7 %copy-done.2 = f32[6,16]{1,0:T(8,128)S(1)} copy-done((f32[6,16]{1,0:T(8,128)S(1)}, f32[6,16]{1,0:T(8,128)}, u32[]{:S(2)}) %copy-start.2) | copy-done | bytes 408
  2.7 0.0 copy-start.3
  2.7 0.7 %copy-done.3 = f32[512]{0:T(512)S(1)} copy-done((f32[512]{0:T(512)S(1)}, f32[512]{0:T(512)}, u32[]{:S(2)}) %copy-start.3) | copy-done | bytes 2072
  3.4 0.0 copy-start.4
  3.4 0.7 %copy-done.4 = s32[2,16]{1,0:T(2,128)S(1)} copy-done((s32[2,16]{1,0:T(2,128)S(1)}, s32[2,16]{1,0:T(2,128)}, u32[]{:S(2)}) %copy-start.4) | copy-done | bytes 152
  4.1 0.0 copy-start.5
  4.1 0.7 copy-done.5
  4.7 0.0 copy-start.6
  4.7 0.7 copy-done.6
  5.4 0.0 copy-start.7
  5.4 0.7 copy-done.7
  6.0 58.8 %cluster_step.1 = (f32[12,16]{1,0:T(8,128)S(1)}, f32[2,1,128,128]{3,2,1,0:T(8,128)S(1)}) custom-call(f32[3,512]{1,0:T(4,128)S(1)} %copy-done, f32[3,512]{1,0:T(4,128)S(1)} %copy-done.1, f32[512]{0:T(512)S(1)} %copy-done.3, f32[6,16]{1,0:T(8,128)S(1)} %copy-done.2, s32[16]{0:T(128)S(1)} %copy-done.5, s32[16]{0:T(128)S(1)} %copy-done.6, s32[16]{0:T(128)S(1)} %copy-done.7, ...), custom_call_target="tpu_custom_call" | custom-call | tf_op jit(solution)/shard_map/cluster_step/pallas_call | solution.py:297
  64.8 0.6 copy.12
  65.4 0.7 copy.13
Async XLA Ops:
  0.6 0.7 %copy-start = (f32[3,512]{1,0:T(4,128)S(1)}, f32[3,512]{1,0:T(4,128)}, u32[]{:S(2)}) copy-start(f32[3,512]{1,0:T(4,128)} %pos_ref.1) | copy-start | bytes 18436
  1.3 0.7 %copy-start.1 = (f32[3,512]{1,0:T(4,128)S(1)}, f32[3,512]{1,0:T(4,128)}, u32[]{:S(2)}) copy-start(f32[3,512]{1,0:T(4,128)} %vel_ref.1) | copy-start | bytes 18436
  2.0 0.7 %copy-start.2 = (f32[6,16]{1,0:T(8,128)S(1)}, f32[6,16]{1,0:T(8,128)}, u32[]{:S(2)}) copy-start(f32[6,16]{1,0:T(8,128)} %old_ref.1) | copy-start | bytes 1156
  2.7 0.7 %copy-start.3 = (f32[512]{0:T(512)S(1)}, f32[512]{0:T(512)}, u32[]{:S(2)}) copy-start(f32[512]{0:T(512)} %mass_ref.1) | copy-start | bytes 6148
  3.4 0.7 %copy-start.4 = (s32[2,16]{1,0:T(2,128)S(1)}, s32[2,16]{1,0:T(2,128)}, u32[]{:S(2)}) copy-start(s32[2,16]{1,0:T(2,128)} %offset_ref.1) | copy-start | bytes 388
  4.1 0.7 copy-start.5
  4.7 0.7 copy-start.6
  5.4 0.7 copy-start.7

commit v2 on v1

v2 whole, which is shorter than its diff:
```python
import functools
import math

import jax
import jax.numpy as jnp
from jax import lax
from jax.experimental import pallas as pl
from jax.experimental.pallas import tpu as pltpu
from jax.sharding import PartitionSpec as P

MESH = pl.DeviceIdType.MESH
F32, BF16 = jnp.float32, jnp.bfloat16
RING = 8
SRC = 512
ACT = 16
LANES = 128
TILE_W = 128


def split3(v):
    a = v.astype(BF16)
    r = v - a.astype(F32)
    b = r.astype(BF16)
    return a, b, (r - b.astype(F32)).astype(BF16)


def wide3(v):
    return [p.astype(F32) for p in split3(v)]


def wide2(v):
    a = v.astype(BF16).astype(F32)
    return a, (v - a).astype(BF16).astype(F32)


def coarse(v):
    return jnp.round(v * 32.0) * (1.0 / 32.0)


def pad_rows(v, rows):
    gap = jnp.zeros((rows - v.shape[0], v.shape[1]), v.dtype)
    return jnp.concatenate([v, gap], axis=0)


def features(pos, vel, soften):
    h, u = coarse(pos), coarse(vel)
    l, m = pos - h, vel - u
    l1, l2 = wide2(l)
    m1, m2 = wide2(m)
    total = lambda v: jnp.sum(v, axis=0, keepdims=True)
    hh = wide3(total(h * h))
    hl = wide3(total(2.0 * h * l + l * l) + (0.0 if soften is None else soften))
    hu = wide3(total(h * u))
    hm = wide3(total(h * m + l * u + l * m))
    ones = [jnp.ones_like(h)]
    if soften is None:
        near = [h] + hh + ones + [h, h, l1, l2, l1, l1, l2] + hl + ones
        dots = [h, u] + hu + ones + [h, h, m1, m2, l1, l2, u, u, l1, l1, l2, m1, m1, m2] + hm + ones
    else:
        near = [-2.0 * h] + ones + hh
        near += [-2.0 * l1, -2.0 * l2, -2.0 * h, -2.0 * h, -2.0 * l1, -2.0 * l2, -2.0 * l1] + ones + hl
        dots = [-u, -h] + ones + hu
        dots += [-m1, -m2, -h, -h, -u, -u, -l1, -l2, -m1, -m2, -m1, -l1, -l2, -l1] + ones + hm
    near = jnp.concatenate(near, axis=0)
    return near.shape[0], pad_rows(jnp.concatenate([near] + dots, axis=0), LANES)


def correct(targets, force, old_accel, level):
    step = jnp.exp2(-level)
    gap = old_accel[0:3] - force[0:3]
    first = -6.0 * gap - step * (4.0 * old_accel[3:6] + 2.0 * force[3:6])
    second = 12.0 * gap + 6.0 * step * (old_accel[3:6] + force[3:6])
    pos = targets[0:3] + step * step * (first / 24.0 + second / 120.0)
    vel = targets[3:6] + step * (first / 6.0 + second / 24.0)
    return jnp.concatenate([pos, vel, force], axis=0)

STEPS = (0, 1, 7, 2, 6, 3, 5, 4)
GROUPS = ((0, 1), (1, 5), (5, 8))


def kernel(
    gravity, soften,
    pos_in, vel_in, mass_in, old_in, index_in, level_in, tile_in, offset_in,
    state_ref, image_ref,
    pos_ref, vel_ref, mass_ref, old_ref, index_ref, level_ref, tile_ref, offset_ref,
    source, small, own, own_in, rest, rest_in, settled, targets, source_f, moments, near_f, dots_f,
    part, part_in, half, half_in, spread, gathered, tiles, tiles_all, left, right,
    load_sem, send_sem, recv_sem,
):
    team, loop = lax.axis_index("team"), lax.axis_index("loop")
    zh, y, c = team // 16, (team // 2) % 8, team % 2
    zl, x = loop // 4, loop % 4
    z = zh * 2 + zl

    def at(y, z, x, c):
        return ((z // 2) * 16 + y * 2 + c, (z % 2) * 4 + x)

    def y_peer(s):
        return at((y + STEPS[s]) % 8, z, x, c)

    def z_peer(s):
        return at(y, (z + STEPS[s]) % 8, x, c)

    def x_peer(s, sign=1):
        return at(y, z, (x + 4 + sign * (s // 2)) % 4, (c + s % 2) % 2)

    slots = range(1, RING)
    barrier = pltpu.get_barrier_semaphore()
    for s in reversed(slots):
        for peer in (y_peer(s), z_peer(s), x_peer(s)):
            pl.semaphore_signal(barrier, inc=1, device_id=peer, device_id_type=MESH)
    loads = [
        pltpu.make_async_copy(src, dst, load_sem.at[i])
        for i, (src, dst) in enumerate(
            (
                (pos_in, pos_ref), (vel_in, vel_ref), (mass_in, mass_ref), (index_in, index_ref),
                (old_in, old_ref), (level_in, level_ref), (tile_in, tile_ref), (offset_in, offset_ref),
            )
        )
    ]
    for one in loads:
        one.start()
    for one in loads:
        one.wait()

    def copy(stage, slot, src, dst, peer):
        return pltpu.make_async_remote_copy(
            src_ref=src,
            dst_ref=dst,
            send_sem=send_sem.at[stage],
            recv_sem=recv_sem.at[stage, slot],
            device_id=peer,
            device_id_type=MESH,
        )

    def await_all(stage, ref):
        copy(stage, 0, ref, ref, y_peer(1)).wait_recv()

    def await_sent(stage, ref):
        copy(stage, 0, ref, ref, y_peer(1)).wait_send()

    source[0, 0:3, :] = pos_ref[...]
    source[0, 3:6, :] = vel_ref[...]
    source[0, 6:7, :] = mass_ref[...].reshape(1, SRC)
    source[0, 7:8, :] = jnp.zeros((1, SRC), F32)
    small[...] = jnp.zeros_like(small)
    small[0:6, 0:ACT] = old_ref[...]
    small[6:7, 0:ACT] = level_ref[...].reshape(1, ACT).astype(F32)
    small[7:8, 0:ACT] = tile_ref[...].reshape(1, ACT).astype(F32)
    small[8:10, 0:ACT] = offset_ref[...].astype(F32)
    small[10:11, 0:ACT] = index_ref[...].reshape(1, ACT).astype(F32)
    placed = pltpu.roll(small[...], y * ACT, 1)
    star = lax.broadcasted_iota(jnp.int32, (SRC, LANES), 0).astype(F32)
    lane = lax.broadcasted_iota(jnp.int32, (SRC, LANES), 1)
    chosen = jnp.where((star == placed[10:11]) & (lane // ACT == y), 1.0, 0.0).astype(BF16)
    pieces = jnp.concatenate(wide3(source[0]), axis=0).astype(BF16)
    picked = jnp.dot(pieces, chosen, preferred_element_type=F32)
    own[...] = picked[0:8] + picked[8:16] + picked[16:24]
    rest[...] = placed

    pl.semaphore_wait(barrier, 3 * (RING - 1))

    for s in reversed(slots):
        copy(0, 0, own, own_in.at[s - 1], y_peer(s)).start()
    for s in reversed(slots):
        copy(2, s, source.at[0], source.at[s], z_peer(s)).start()
    for s in slots:
        copy(1, 0, rest, rest_in.at[s - 1], y_peer(s)).start()

    def prepare_source(s):
        v = source[s]
        rows = slice(s * SRC, (s + 1) * SRC)
        source_f[rows, :] = jnp.transpose(features(v[0:3], v[3:6], None)[1]).astype(BF16)
        mass = v[6:7]
        sums = jnp.concatenate([v[0:3] * mass, v[3:6] * mass, mass, jnp.zeros_like(mass)], axis=0)
        moments[:, rows] = pad_rows(jnp.concatenate(wide3(sums), axis=0), 32).astype(BF16)

    def await_source(s):
        copy(2, s, source.at[0], source.at[s], z_peer(s)).wait_recv()

    prepare_source(0)
    for s in range(1, 5):
        await_source(s)
        prepare_source(s)

    await_all(0, own_in)
    block = own[...]
    for s in slots:
        block = block + own_in[s - 1]
    targets[0] = block
    for s in (4, 5, 2, 3, 6, 7, 1):
        copy(3, s, targets.at[0], targets.at[s], x_peer(s)).start()

    def prepare_targets(first, last):
        t = jnp.concatenate([targets[s] for s in range(first, last)], axis=1)
        cut, f = features(t[0:3], t[3:6], soften)
        row = lax.broadcasted_iota(jnp.int32, f.shape, 0)
        lanes = slice(first * LANES, last * LANES)
        near_f[:, lanes] = jnp.where(row < cut, f, 0.0).astype(BF16)
        dots_f[:, lanes] = jnp.where(row < cut, 0.0, f).astype(BF16)

    prepare_targets(0, 1)
    for s in range(5, RING):
        await_source(s)
        prepare_source(s)

    def forces(s):
        lanes = pl.ds(pl.multiple_of(s * LANES, LANES), LANES)
        dist_sq = jnp.dot(source_f[...], near_f[:, lanes], preferred_element_type=F32)
        dots = jnp.dot(source_f[...], dots_f[:, lanes], preferred_element_type=F32)
        inverse = lax.rsqrt(dist_sq)
        inverse_sq = inverse * inverse
        strength = inverse * inverse_sq
        radial = (strength * inverse_sq) * dots
        plain = jnp.dot(moments[...], strength.astype(BF16), preferred_element_type=F32)
        tilted = jnp.dot(moments[...], radial.astype(BF16), preferred_element_type=F32)
        plain = plain[0:8] + plain[8:16] + plain[16:24]
        tilted = tilted[0:8] + tilted[8:16] + tilted[16:24]
        t = targets[s]
        accel = plain[0:3] - t[0:3] * plain[6:7]
        jerk = (plain[3:6] - t[3:6] * plain[6:7]) - 3.0 * (tilted[0:3] - t[0:3] * tilted[6:7])
        part[s] = pad_rows(gravity * jnp.concatenate([accel, jerk], axis=0), 8)

    forces(0)

    await_all(1, rest_in)
    others = rest[...]
    for s in slots:
        others = others + rest_in[s - 1]
    settled[...] = others
    tiles[0] = others[7:8]
    for s in slots:
        copy(10, 0, tiles.at[0], tiles.at[s], z_peer(s)).start()

    for s in slots:
        copy(3, s, targets.at[0], targets.at[s], x_peer(s)).wait_recv()
    prepare_targets(1, RING)

    def force_step(i, carry):
        s = jnp.where(i == 7, 1, jnp.where(i < 3, i + 3, jnp.where(i < 5, i - 1, i + 1)))
        forces(s)
        copy(4, s, part.at[s], part_in.at[s], x_peer(s, -1)).start()
        return carry

    lax.fori_loop(1, RING, force_step, 0)

    await_all(10, tiles.at[pl.ds(1, RING - 1)])
    for s in slots:
        copy(11, 0, tiles, tiles_all.at[s - 1], x_peer(s)).start()

    total = part[0]
    for s in (4, 5, 2, 3, 6, 7, 1):
        copy(4, s, part.at[s], part_in.at[s], x_peer(s, -1)).wait_recv()
        total = total + part_in[s]
    half[...] = total
    for s in reversed(slots):
        copy(5, 0, half, half_in.at[s - 1], y_peer(s)).start()
    await_sent(0, own_in)
    await_sent(1, rest_in)
    await_sent(2, source.at[pl.ds(1, RING - 1)])
    await_sent(3, targets.at[pl.ds(1, RING - 1)])
    await_sent(4, part.at[pl.ds(1, RING - 1)])
    await_sent(10, tiles.at[pl.ds(1, RING - 1)])
    await_sent(11, tiles_all)
    await_all(11, tiles_all)
    await_all(5, half_in)
    for s in slots:
        total = total + half_in[s - 1]

    stars = targets[0]
    others = settled[...]
    state = correct(stars[0:6], total[0:6], others[0:6], others[6:7])
    centre_y = others[8:9] + (TILE_W / 16.0) * jnp.tanh(state[1:2])
    centre_x = others[9:10] + (TILE_W / 16.0) * jnp.tanh(state[0:1])
    mass = stars[6:7]
    spread[0] = jnp.concatenate([mass, mass * state[5:6] * state[5:6], centre_y, centre_x], axis=0)
    for s in reversed(slots):
        copy(6, s, spread.at[0], spread.at[s], z_peer(s)).start()

    def group(g, s, peer):
        low, high = GROUPS[g]
        piece = pl.ds(low, high - low)
        return copy(7 + g, s, spread.at[piece], gathered.at[s, piece], peer)

    def forward(g):
        for s in (4, 5, 2, 3, 6, 7, 1):
            group(g, s, x_peer(s)).start()

    def await_spread(low, high):
        for s in range(low, high):
            copy(6, s, spread.at[0], spread.at[s], z_peer(s)).wait_recv()

    mine = (team * 8 + loop).astype(F32)
    reach = (40.0 / TILE_W) * math.sqrt(0.5 * math.log2(math.e))
    cell = (lax.broadcasted_iota(jnp.int32, (TILE_W, LANES), 0).astype(F32) + 0.5) * reach

    def kernel_of(centre):
        scaled = cell - centre * reach
        return jnp.exp2(-(scaled * scaled))

    def add_stars(blocks, first=False):
        for b, (rows, tile) in enumerate(blocks):
            here = tile == mine
            rows_y, rows_x = kernel_of(rows[2:3]), kernel_of(rows[3:4])
            lanes = slice(b * LANES, (b + 1) * LANES)
            left[0:TILE_W, lanes] = (jnp.where(here, rows[0:1], 0.0) * rows_y).astype(BF16)
            left[TILE_W:, lanes] = (jnp.where(here, rows[1:2], 0.0) * rows_y).astype(BF16)
            right[:, lanes] = rows_x.astype(BF16)
        depth = len(blocks) * LANES
        out = lax.dot_general(
            left[:, 0:depth], right[:, 0:depth], (((1,), (1,)), ((), ())), preferred_element_type=F32
        ).reshape(2, 1, TILE_W, TILE_W)
        if first:
            image_ref[...] = out
        else:
            image_ref[...] += out

    def mine_of(low, high):
        return [(spread[s], tiles[s]) for s in range(low, high)]

    forward(0)
    shifted = pltpu.roll(pad_rows(state, 16), (LANES - y * ACT) % LANES, 1)
    state_ref[...] = shifted[0:12, 0:ACT]
    add_stars(mine_of(0, 1), True)
    await_spread(1, 5)
    forward(1)
    add_stars(mine_of(1, 5))
    await_spread(5, RING)
    forward(2)
    add_stars(mine_of(5, RING))
    for s in (1, 2, 3, 6, 7, 4, 5):
        group(0, s, x_peer(s)).wait_recv()
    add_stars([(gathered[s, 0], tiles_all[s - 1, 0]) for s in slots])

    def deposit_step(g):
        low, high = GROUPS[g]

        def step(s, carry):
            group(g, s, x_peer(s)).wait_recv()
            add_stars([(gathered[s, k], tiles_all[s - 1, k]) for k in range(low, high)])
            return carry

        return step

    lax.fori_loop(1, RING, deposit_step(1), 0)
    lax.fori_loop(1, RING, deposit_step(2), 0)
    await_sent(5, half_in)
    await_sent(6, spread.at[pl.ds(1, RING - 1)])
    for g, (low, high) in enumerate(GROUPS):
        await_sent(7 + g, gathered.at[pl.ds(1, RING - 1), pl.ds(low, high - low)])


def shards(*arrays):
    stars = SRC * RING**3
    stage_count = 12
    vmem = pl.BlockSpec(memory_space=pltpu.VMEM)
    return pl.pallas_call(
        functools.partial(kernel, 1.0 / stars, float(stars) ** (-2.0 / 3.0)),
        out_shape=(
            jax.ShapeDtypeStruct((12, ACT), F32),
            jax.ShapeDtypeStruct((2, 1, TILE_W, TILE_W), F32),
        ),
        in_specs=[pl.BlockSpec(memory_space=pl.ANY)] * len(arrays),
        out_specs=(vmem, vmem),
        scratch_shapes=[pltpu.VMEM(v.shape, v.dtype) for v in arrays] + [
            pltpu.VMEM((RING, 8, SRC), F32),
            pltpu.VMEM((16, LANES), F32),
            pltpu.VMEM((8, LANES), F32),
            pltpu.VMEM((RING - 1, 8, LANES), F32),
            pltpu.VMEM((16, LANES), F32),
            pltpu.VMEM((RING - 1, 16, LANES), F32),
            pltpu.VMEM((16, LANES), F32),
            pltpu.VMEM((RING, 8, LANES), F32),
            pltpu.VMEM((RING * SRC, LANES), BF16),
            pltpu.VMEM((32, RING * SRC), BF16),
            pltpu.VMEM((LANES, RING * LANES), BF16),
            pltpu.VMEM((LANES, RING * LANES), BF16),
            pltpu.VMEM((RING, 8, LANES), F32),
            pltpu.VMEM((RING, 8, LANES), F32),
            pltpu.VMEM((8, LANES), F32),
            pltpu.VMEM((RING - 1, 8, LANES), F32),
            pltpu.VMEM((RING, 4, LANES), F32),
            pltpu.VMEM((RING, RING, 4, LANES), F32),
            pltpu.VMEM((RING, 1, LANES), F32),
            pltpu.VMEM((RING - 1, RING, 1, LANES), F32),
            pltpu.VMEM((2 * TILE_W, RING * LANES), BF16),
            pltpu.VMEM((TILE_W, RING * LANES), BF16),
            pltpu.SemaphoreType.DMA((len(arrays),)),
            pltpu.SemaphoreType.DMA((stage_count,)),
            pltpu.SemaphoreType.DMA((stage_count, RING)),
        ],
        compiler_params=pltpu.CompilerParams(
            collective_id=0, has_side_effects=True, vmem_limit_bytes=60 << 20
        ),
        name="cluster_step",
    )(*arrays)


def solution(mesh):
    both = ("team", "loop")
    columns, rows = P(None, both), P(both)
    return jax.shard_map(
        shards,
        mesh=mesh,
        in_specs=(columns, columns, rows, columns, rows, rows, rows, columns),
        out_specs=(columns, P(None, both, None, None)),
        check_vma=False,
    )
```

time: 66.4 us -> 52.2 us (0.79)
  Pallas kernels: 58.8 us -> 48.5 us
  local copies, waits for them, and re-layouts: 6.65 us -> 2.86 us
    pallas_call x1, Pallas kernels: 58.8 us -> 48.5 us  [shards(): pl.pallas_call(functools.partial(kernel, 1.0 / stars, float(stars) ** (-2...]
    unnamed x18 -> x2, local copies, waits for them, and re-layouts: 6.65 us -> 2.86 us
where the time goes in v2:
time: 52.2 us; the launch traced here: 52 us
  Pallas kernels  48.5 us (93%)
  local copies, waits for them, and re-layouts  2.86 us (5%)
  between operations  0.64 us (1%)
    pallas_call x1, Pallas kernels, shards(): pl.pallas_call(functools.partial(kernel, 1.0 / stars, float(stars) ** (-2...  48.5 us
    unnamed x2, local copies, waits for them, and re-layouts  2.86 us

profile of v2, /device:TPU:1, one launch (start us, length us, event | category | flops | bytes accessed | tf_op | source)
XLA Modules:
  0.0 52.0 jit_solution(16852538820667890622)
XLA Ops:
  0.6 48.5 %cluster_step.1 = (f32[12,16]{1,0:T(8,128)}, f32[2,1,128,128]{3,2,1,0:T(8,128)}) custom-call(f32[3,512]{1,0:T(4,128)} %pos_in.1, f32[3,512]{1,0:T(4,128)} %vel_in.1, f32[512]{0:T(512)} %mass_in.1, f32[6,16]{1,0:T(8,128)} %old_in.1, s32[16]{0:T(128)} %index_in.1, s32[16]{0:T(128)} %level_in.1, s32[16]{0:T(128)} %tile_in.1, s32[2,16]{1,0:T(2,128)} %offset_in.1), custom_call_target="tpu_custom_call" | custom-call | tf_op jit(solution)/shard_map/cluster_step/pallas_call | solution.py:357
  49.1 1.3 %copy.12 = f32[12,16]{1,0:T(8,128)} copy(f32[12,16]{1,0:T(8,128)} %get-tuple-element.4) | data formatting | bytes 1536
  50.4 1.6 %copy.13 = f32[2,1,128,128]{3,2,1,0:T(8,128)} copy(f32[2,1,128,128]{3,2,1,0:T(8,128)} %get-tuple-element.5) | data formatting | bytes 262144

commit v3 on v2

--- a/solution.py
+++ b/solution.py
@@ -74,8 +74,8 @@
     vel = targets[3:6] + step * (first / 6.0 + second / 24.0)
     return jnp.concatenate([pos, vel, force], axis=0)
 
-STEPS = (0, 1, 7, 2, 6, 3, 5, 4)
-GROUPS = ((0, 1), (1, 5), (5, 8))
+PAIR = 2
+EARLY = 5
 
 
 def kernel(
@@ -95,14 +95,18 @@
     def at(y, z, x, c):
         return ((z // 2) * 16 + y * 2 + c, (z % 2) * 4 + x)
 
-    def y_peer(s):
-        return at((y + STEPS[s]) % 8, z, x, c)
+    def step_of(s):
+        away = (s + 1) // 2
+        return away + (s + 1) % 2 * (8 - 2 * away)
+
+    def y_peer(s, sign=1):
+        return at((y + 8 + sign * step_of(s)) % 8, z, x, c)
 
     def z_peer(s):
-        return at(y, (z + STEPS[s]) % 8, x, c)
-
-    def x_peer(s, sign=1):
-        return at(y, z, (x + 4 + sign * (s // 2)) % 4, (c + s % 2) % 2)
+        return at(y, (z + step_of(s)) % 8, x, c)
+
+    def x_peer(s):
+        return at(y, z, (x + s // 2) % 4, (c + s % 2) % 2)
 
     slots = range(1, RING)
     barrier = pltpu.get_barrier_semaphore()
@@ -149,10 +153,11 @@
     small[7:8, 0:ACT] = tile_ref[...].reshape(1, ACT).astype(F32)
     small[8:10, 0:ACT] = offset_ref[...].astype(F32)
     small[10:11, 0:ACT] = index_ref[...].reshape(1, ACT).astype(F32)
-    placed = pltpu.roll(small[...], y * ACT, 1)
+    place = x * 2 + c
+    placed = pltpu.roll(small[...], place * ACT, 1)
     star = lax.broadcasted_iota(jnp.int32, (SRC, LANES), 0).astype(F32)
     lane = lax.broadcasted_iota(jnp.int32, (SRC, LANES), 1)
-    chosen = jnp.where((star == placed[10:11]) & (lane // ACT == y), 1.0, 0.0).astype(BF16)
+    chosen = jnp.where((star == placed[10:11]) & (lane // ACT == place), 1.0, 0.0).astype(BF16)
     pieces = jnp.concatenate(wide3(source[0]), axis=0).astype(BF16)
     picked = jnp.dot(pieces, chosen, preferred_element_type=F32)
     own[...] = picked[0:8] + picked[8:16] + picked[16:24]
@@ -160,12 +165,12 @@
 
     pl.semaphore_wait(barrier, 3 * (RING - 1))
 
-    for s in reversed(slots):
-        copy(0, 0, own, own_in.at[s - 1], y_peer(s)).start()
+    for s in (4, 5, 2, 3, 6, 7, 1):
+        copy(0, 0, own, own_in.at[s - 1], x_peer(s)).start()
     for s in reversed(slots):
         copy(2, s, source.at[0], source.at[s], z_peer(s)).start()
     for s in slots:
-        copy(1, 0, rest, rest_in.at[s - 1], y_peer(s)).start()
+        copy(1, 0, rest, rest_in.at[s - 1], x_peer(s)).start()
 
     def prepare_source(s):
         v = source[s]
@@ -178,19 +183,6 @@
     def await_source(s):
         copy(2, s, source.at[0], source.at[s], z_peer(s)).wait_recv()
 
-    prepare_source(0)
-    for s in range(1, 5):
-        await_source(s)
-        prepare_source(s)
-
-    await_all(0, own_in)
-    block = own[...]
-    for s in slots:
-        block = block + own_in[s - 1]
-    targets[0] = block
-    for s in (4, 5, 2, 3, 6, 7, 1):
-        copy(3, s, targets.at[0], targets.at[s], x_peer(s)).start()
-
     def prepare_targets(first, last):
         t = jnp.concatenate([targets[s] for s in range(first, last)], axis=1)
         cut, f = features(t[0:3], t[3:6], soften)
@@ -199,29 +191,39 @@
         near_f[:, lanes] = jnp.where(row < cut, f, 0.0).astype(BF16)
         dots_f[:, lanes] = jnp.where(row < cut, 0.0, f).astype(BF16)
 
-    prepare_targets(0, 1)
-    for s in range(5, RING):
-        await_source(s)
-        prepare_source(s)
-
-    def forces(s):
+    def force_sums(s, first, last):
         lanes = pl.ds(pl.multiple_of(s * LANES, LANES), LANES)
-        dist_sq = jnp.dot(source_f[...], near_f[:, lanes], preferred_element_type=F32)
-        dots = jnp.dot(source_f[...], dots_f[:, lanes], preferred_element_type=F32)
+        rows = slice(first * SRC, last * SRC)
+        dist_sq = jnp.dot(source_f[rows, :], near_f[:, lanes], preferred_element_type=F32)
+        dots = jnp.dot(source_f[rows, :], dots_f[:, lanes], preferred_element_type=F32)
         inverse = lax.rsqrt(dist_sq)
         inverse_sq = inverse * inverse
         strength = inverse * inverse_sq
         radial = (strength * inverse_sq) * dots
-        plain = jnp.dot(moments[...], strength.astype(BF16), preferred_element_type=F32)
-        tilted = jnp.dot(moments[...], radial.astype(BF16), preferred_element_type=F32)
-        plain = plain[0:8] + plain[8:16] + plain[16:24]
-        tilted = tilted[0:8] + tilted[8:16] + tilted[16:24]
+        plain = jnp.dot(moments[:, rows], strength.astype(BF16), preferred_element_type=F32)
+        tilted = jnp.dot(moments[:, rows], radial.astype(BF16), preferred_element_type=F32)
+        return plain[0:8] + plain[8:16] + plain[16:24], tilted[0:8] + tilted[8:16] + tilted[16:24]
+
+    def combine(s, plain, tilted):
         t = targets[s]
         accel = plain[0:3] - t[0:3] * plain[6:7]
         jerk = (plain[3:6] - t[3:6] * plain[6:7]) - 3.0 * (tilted[0:3] - t[0:3] * tilted[6:7])
         part[s] = pad_rows(gravity * jnp.concatenate([accel, jerk], axis=0), 8)
 
-    forces(0)
+    prepare_source(0)
+
+    await_all(0, own_in)
+    block = own[...]
+    for s in slots:
+        block = block + own_in[s - 1]
+    targets[0] = block
+    for s in reversed(slots):
+        copy(3, s, targets.at[0], targets.at[s], y_peer(s)).start()
+    prepare_targets(0, 1)
+    for s in range(1, EARLY):
+        await_source(s)
+        prepare_source(s)
+    plain, tilted = force_sums(0, 0, EARLY)
 
     await_all(1, rest_in)
     others = rest[...]
@@ -230,39 +232,62 @@
     settled[...] = others
     tiles[0] = others[7:8]
     for s in slots:
-        copy(10, 0, tiles.at[0], tiles.at[s], z_peer(s)).start()
-
-    for s in slots:
-        copy(3, s, targets.at[0], targets.at[s], x_peer(s)).wait_recv()
-    prepare_targets(1, RING)
+        copy(11, 0, tiles.at[0], tiles.at[s], z_peer(s)).start()
+    image_ref[...] = jnp.zeros_like(image_ref)
+
+    for s in range(EARLY, RING):
+        await_source(s)
+        prepare_source(s)
+    more = force_sums(0, EARLY, RING)
+    combine(0, plain + more[0], tilted + more[1])
+
+    def await_targets(s):
+        copy(3, s, targets.at[0], targets.at[s], y_peer(s)).wait_recv()
 
     def force_step(i, carry):
-        s = jnp.where(i == 7, 1, jnp.where(i < 3, i + 3, jnp.where(i < 5, i - 1, i + 1)))
-        forces(s)
-        copy(4, s, part.at[s], part_in.at[s], x_peer(s, -1)).start()
+        @pl.when(i == 0)
+        def _():
+            await_targets(1)
+            prepare_targets(1, 2)
+
+        @pl.when(i == 1)
+        def _():
+            await_targets(3)
+            prepare_targets(3, 4)
+
+        @pl.when(i == 2)
+        def _():
+            for s in (2, 4, 5, 6, 7):
+                await_targets(s)
+            prepare_targets(4, RING)
+            prepare_targets(2, 3)
+
+        s = jnp.where(i < 2, 2 * i + 1, jnp.where(i == 2, 7, jnp.where(i == 3, 5, 14 - 2 * i)))
+        combine(s, *force_sums(s, 0, RING))
+        copy(4, s, part.at[s], part_in.at[s], y_peer(s, -1)).start()
         return carry
 
-    lax.fori_loop(1, RING, force_step, 0)
-
-    await_all(10, tiles.at[pl.ds(1, RING - 1)])
-    for s in slots:
-        copy(11, 0, tiles, tiles_all.at[s - 1], x_peer(s)).start()
+    lax.fori_loop(0, RING - 1, force_step, 0)
+
+    await_all(11, tiles.at[pl.ds(1, RING - 1)])
+    for s in slots:
+        copy(12, 0, tiles, tiles_all.at[s - 1], y_peer(s)).start()
 
     total = part[0]
-    for s in (4, 5, 2, 3, 6, 7, 1):
-        copy(4, s, part.at[s], part_in.at[s], x_peer(s, -1)).wait_recv()
+    for s in (1, 3, 7, 5, 6, 4, 2):
+        copy(4, s, part.at[s], part_in.at[s], y_peer(s, -1)).wait_recv()
         total = total + part_in[s]
     half[...] = total
-    for s in reversed(slots):
-        copy(5, 0, half, half_in.at[s - 1], y_peer(s)).start()
+    for s in (4, 5, 2, 3, 6, 7, 1):
+        copy(5, 0, half, half_in.at[s - 1], x_peer(s)).start()
     await_sent(0, own_in)
     await_sent(1, rest_in)
     await_sent(2, source.at[pl.ds(1, RING - 1)])
     await_sent(3, targets.at[pl.ds(1, RING - 1)])
     await_sent(4, part.at[pl.ds(1, RING - 1)])
-    await_sent(10, tiles.at[pl.ds(1, RING - 1)])
-    await_sent(11, tiles_all)
-    await_all(11, tiles_all)
+    await_sent(11, tiles.at[pl.ds(1, RING - 1)])
+    await_sent(12, tiles_all)
+    await_all(12, tiles_all)
     await_all(5, half_in)
     for s in slots:
         total = total + half_in[s - 1]
@@ -277,18 +302,9 @@
     for s in reversed(slots):
         copy(6, s, spread.at[0], spread.at[s], z_peer(s)).start()
 
-    def group(g, s, peer):
-        low, high = GROUPS[g]
-        piece = pl.ds(low, high - low)
+    def pair(g, s, peer):
+        piece = pl.ds(g * PAIR, PAIR)
         return copy(7 + g, s, spread.at[piece], gathered.at[s, piece], peer)
-
-    def forward(g):
-        for s in (4, 5, 2, 3, 6, 7, 1):
-            group(g, s, x_peer(s)).start()
-
-    def await_spread(low, high):
-        for s in range(low, high):
-            copy(6, s, spread.at[0], spread.at[s], z_peer(s)).wait_recv()
 
     mine = (team * 8 + loop).astype(F32)
     reach = (40.0 / TILE_W) * math.sqrt(0.5 * math.log2(math.e))
@@ -298,7 +314,7 @@
         scaled = cell - centre * reach
         return jnp.exp2(-(scaled * scaled))
 
-    def add_stars(blocks, first=False):
+    def add_stars(blocks):
         for b, (rows, tile) in enumerate(blocks):
             here = tile == mine
             rows_y, rows_x = kernel_of(rows[2:3]), kernel_of(rows[3:4])
@@ -306,53 +322,51 @@
             left[0:TILE_W, lanes] = (jnp.where(here, rows[0:1], 0.0) * rows_y).astype(BF16)
             left[TILE_W:, lanes] = (jnp.where(here, rows[1:2], 0.0) * rows_y).astype(BF16)
             right[:, lanes] = rows_x.astype(BF16)
-        depth = len(blocks) * LANES
         out = lax.dot_general(
-            left[:, 0:depth], right[:, 0:depth], (((1,), (1,)), ((), ())), preferred_element_type=F32
-        ).reshape(2, 1, TILE_W, TILE_W)
-        if first:
-            image_ref[...] = out
-        else:
-            image_ref[...] += out
-
-    def mine_of(low, high):
-        return [(spread[s], tiles[s]) for s in range(low, high)]
-
-    forward(0)
-    shifted = pltpu.roll(pad_rows(state, 16), (LANES - y * ACT) % LANES, 1)
+            left[...], right[...], (((1,), (1,)), ((), ())), preferred_element_type=F32
+        )
+        image_ref[...] += out.reshape(2, 1, TILE_W, TILE_W)
+
+    def forward_step(g, carry):
+        @pl.when(g == 0)
+        def _():
+            copy(6, 1, spread.at[0], spread.at[1], z_peer(1)).wait_recv()
+
+        @pl.when(g > 0)
+        def _():
+            for s in (2 * g, 2 * g + 1):
+                copy(6, s, spread.at[0], spread.at[s], z_peer(s)).wait_recv()
+
+        for s in reversed(slots):
+            pair(g, s, y_peer(s)).start()
+        add_stars([(spread[g * PAIR + k], tiles[g * PAIR + k]) for k in range(PAIR)])
+        return carry
+
+    shifted = pltpu.roll(pad_rows(state, 16), (LANES - place * ACT) % LANES, 1)
     state_ref[...] = shifted[0:12, 0:ACT]
-    add_stars(mine_of(0, 1), True)
-    await_spread(1, 5)
-    forward(1)
-    add_stars(mine_of(1, 5))
-    await_spread(5, RING)
-    forward(2)
-    add_stars(mine_of(5, RING))
-    for s in (1, 2, 3, 6, 7, 4, 5):
-        group(0, s, x_peer(s)).wait_recv()
-    add_stars([(gathered[s, 0], tiles_all[s - 1, 0]) for s in slots])
-
-    def deposit_step(g):
-        low, high = GROUPS[g]
-
-        def step(s, carry):
-            group(g, s, x_peer(s)).wait_recv()
-            add_stars([(gathered[s, k], tiles_all[s - 1, k]) for k in range(low, high)])
-            return carry
-
-        return step
-
-    lax.fori_loop(1, RING, deposit_step(1), 0)
-    lax.fori_loop(1, RING, deposit_step(2), 0)
+    lax.fori_loop(0, RING // PAIR, forward_step, 0)
+
+    def deposit_step(i, carry):
+        late, s = i // (RING - 1) + 1, i % (RING - 1) + 1
+        g = late - (s + 1) // 2
+
+        @pl.when((g >= 0) & (g < RING // PAIR))
+        def _():
+            pair(g, s, y_peer(s)).wait_recv()
+            add_stars([(gathered[s, g * PAIR + k], tiles_all[s - 1, g * PAIR + k]) for k in range(PAIR)])
+
+        return carry
+
+    lax.fori_loop(0, (RING - 1) * (RING - 1), deposit_step, 0)
     await_sent(5, half_in)
     await_sent(6, spread.at[pl.ds(1, RING - 1)])
-    for g, (low, high) in enumerate(GROUPS):
-        await_sent(7 + g, gathered.at[pl.ds(1, RING - 1), pl.ds(low, high - low)])
+    for g in range(RING // PAIR):
+        await_sent(7 + g, gathered.at[pl.ds(1, RING - 1), pl.ds(g * PAIR, PAIR)])
 
 
 def shards(*arrays):
     stars = SRC * RING**3
-    stage_count = 12
+    stage_count = 13
     vmem = pl.BlockSpec(memory_space=pltpu.VMEM)
     return pl.pallas_call(
         functools.partial(kernel, 1.0 / stars, float(stars) ** (-2.0 / 3.0)),
@@ -383,8 +397,8 @@
             pltpu.VMEM((RING, RING, 4, LANES), F32),
             pltpu.VMEM((RING, 1, LANES), F32),
             pltpu.VMEM((RING - 1, RING, 1, LANES), F32),
-            pltpu.VMEM((2 * TILE_W, RING * LANES), BF16),
-            pltpu.VMEM((TILE_W, RING * LANES), BF16),
+            pltpu.VMEM((2 * TILE_W, PAIR * LANES), BF16),
+            pltpu.VMEM((TILE_W, PAIR * LANES), BF16),
             pltpu.SemaphoreType.DMA((len(arrays),)),
             pltpu.SemaphoreType.DMA((stage_count,)),
             pltpu.SemaphoreType.DMA((stage_count, RING)),

time: 52.2 us -> 52.7 us (level)
  no operation moved by 1% of the time
where the time goes in v3:
time: 52.7 us; the launch traced here: 52.5 us
  Pallas kernels  49 us (93%)
  local copies, waits for them, and re-layouts  2.86 us (5%)
  between operations  0.64 us (1%)
    pallas_call x1, Pallas kernels, shards(): pl.pallas_call(functools.partial(kernel, 1.0 / stars, float(stars) ** (-2...  49 us
    unnamed x2, local copies, waits for them, and re-layouts  2.86 us

profile of v3, /device:TPU:1, one launch (start us, length us, event | category | flops | bytes accessed | tf_op | source)
XLA Modules:
  0.0 52.5 jit_solution(16489355959732376754)
XLA Ops:
  0.6 49.0 %cluster_step.1 = (f32[12,16]{1,0:T(8,128)}, f32[2,1,128,128]{3,2,1,0:T(8,128)}) custom-call(f32[3,512]{1,0:T(4,128)} %pos_in.1, f32[3,512]{1,0:T(4,128)} %vel_in.1, f32[512]{0:T(512)} %mass_in.1, f32[6,16]{1,0:T(8,128)} %old_in.1, s32[16]{0:T(128)} %index_in.1, s32[16]{0:T(128)} %level_in.1, s32[16]{0:T(128)} %tile_in.1, s32[2,16]{1,0:T(2,128)} %offset_in.1), custom_call_target="tpu_custom_call" | custom-call | tf_op jit(solution)/shard_map/cluster_step/pallas_call | solution.py:371
  49.6 1.3 %copy.12 = f32[12,16]{1,0:T(8,128)} copy(f32[12,16]{1,0:T(8,128)} %get-tuple-element.4) | data formatting | bytes 1536
  50.9 1.6 %copy.13 = f32[2,1,128,128]{3,2,1,0:T(8,128)} copy(f32[2,1,128,128]{3,2,1,0:T(8,128)} %get-tuple-element.5) | data formatting | bytes 262144

commit v4 on v3

--- a/solution.py
+++ b/solution.py
@@ -74,7 +74,7 @@
     vel = targets[3:6] + step * (first / 6.0 + second / 24.0)
     return jnp.concatenate([pos, vel, force], axis=0)
 
-PAIR = 2
+FOUR = 4
 EARLY = 5
 
 
@@ -262,16 +262,18 @@
             prepare_targets(4, RING)
             prepare_targets(2, 3)
 
+        @pl.when(i == 3)
+        def _():
+            await_all(11, tiles.at[pl.ds(1, RING - 1)])
+            for s in slots:
+                copy(12, 0, tiles, tiles_all.at[s - 1], y_peer(s)).start()
+
         s = jnp.where(i < 2, 2 * i + 1, jnp.where(i == 2, 7, jnp.where(i == 3, 5, 14 - 2 * i)))
         combine(s, *force_sums(s, 0, RING))
         copy(4, s, part.at[s], part_in.at[s], y_peer(s, -1)).start()
         return carry
 
     lax.fori_loop(0, RING - 1, force_step, 0)
-
-    await_all(11, tiles.at[pl.ds(1, RING - 1)])
-    for s in slots:
-        copy(12, 0, tiles, tiles_all.at[s - 1], y_peer(s)).start()
 
     total = part[0]
     for s in (1, 3, 7, 5, 6, 4, 2):
@@ -302,8 +304,8 @@
     for s in reversed(slots):
         copy(6, s, spread.at[0], spread.at[s], z_peer(s)).start()
 
-    def pair(g, s, peer):
-        piece = pl.ds(g * PAIR, PAIR)
+    def four(g, s, peer):
+        piece = pl.ds(g * FOUR, FOUR)
         return copy(7 + g, s, spread.at[piece], gathered.at[s, piece], peer)
 
     mine = (team * 8 + loop).astype(F32)
@@ -327,53 +329,54 @@
         )
         image_ref[...] += out.reshape(2, 1, TILE_W, TILE_W)
 
-    def forward_step(g, carry):
-        @pl.when(g == 0)
-        def _():
-            copy(6, 1, spread.at[0], spread.at[1], z_peer(1)).wait_recv()
-
-        @pl.when(g > 0)
-        def _():
-            for s in (2 * g, 2 * g + 1):
-                copy(6, s, spread.at[0], spread.at[s], z_peer(s)).wait_recv()
-
+    def forward(g):
+        for s in range(max(1, g * FOUR), (g + 1) * FOUR):
+            copy(6, s, spread.at[0], spread.at[s], z_peer(s)).wait_recv()
         for s in reversed(slots):
-            pair(g, s, y_peer(s)).start()
-        add_stars([(spread[g * PAIR + k], tiles[g * PAIR + k]) for k in range(PAIR)])
-        return carry
+            four(g, s, y_peer(s)).start()
+        add_stars([(spread[g * FOUR + k], tiles[g * FOUR + k]) for k in range(FOUR)])
 
     shifted = pltpu.roll(pad_rows(state, 16), (LANES - place * ACT) % LANES, 1)
     state_ref[...] = shifted[0:12, 0:ACT]
-    lax.fori_loop(0, RING // PAIR, forward_step, 0)
+    forward(0)
+    forward(1)
 
     def deposit_step(i, carry):
-        late, s = i // (RING - 1) + 1, i % (RING - 1) + 1
-        g = late - (s + 1) // 2
-
-        @pl.when((g >= 0) & (g < RING // PAIR))
-        def _():
-            pair(g, s, y_peer(s)).wait_recv()
-            add_stars([(gathered[s, g * PAIR + k], tiles_all[s - 1, g * PAIR + k]) for k in range(PAIR)])
-
+        g = jnp.where((i < 6) | (i == 8), 0, 1)
+        s = jnp.where(i < 6, i + 1, jnp.where(i < 8, i - 5, jnp.where(i == 8, 7, i - 6)))
+        four(g, s, y_peer(s)).wait_recv()
+        add_stars([(gathered[s, g * FOUR + k], tiles_all[s - 1, g * FOUR + k]) for k in range(FOUR)])
         return carry
 
-    lax.fori_loop(0, (RING - 1) * (RING - 1), deposit_step, 0)
+    lax.fori_loop(0, 2 * (RING - 1), deposit_step, 0)
     await_sent(5, half_in)
     await_sent(6, spread.at[pl.ds(1, RING - 1)])
-    for g in range(RING // PAIR):
-        await_sent(7 + g, gathered.at[pl.ds(1, RING - 1), pl.ds(g * PAIR, PAIR)])
+    for g in range(RING // FOUR):
+        await_sent(7 + g, gathered.at[pl.ds(1, RING - 1), pl.ds(g * FOUR, FOUR)])
+
+
+def store(state_in, image_in, state_out, image_out, sem):
+    copies = [
+        pltpu.make_async_copy(state_in, state_out, sem.at[0]),
+        pltpu.make_async_copy(image_in, image_out, sem.at[1]),
+    ]
+    for one in reversed(copies):
+        one.start()
+    for one in copies:
+        one.wait()
 
 
 def shards(*arrays):
     stars = SRC * RING**3
     stage_count = 13
     vmem = pl.BlockSpec(memory_space=pltpu.VMEM)
-    return pl.pallas_call(
+    outputs = (
+        jax.ShapeDtypeStruct((12, ACT), F32),
+        jax.ShapeDtypeStruct((2, 1, TILE_W, TILE_W), F32),
+    )
+    results = pl.pallas_call(
         functools.partial(kernel, 1.0 / stars, float(stars) ** (-2.0 / 3.0)),
-        out_shape=(
-            jax.ShapeDtypeStruct((12, ACT), F32),
-            jax.ShapeDtypeStruct((2, 1, TILE_W, TILE_W), F32),
-        ),
+        out_shape=outputs,
         in_specs=[pl.BlockSpec(memory_space=pl.ANY)] * len(arrays),
         out_specs=(vmem, vmem),
         scratch_shapes=[pltpu.VMEM(v.shape, v.dtype) for v in arrays] + [
@@ -397,8 +400,8 @@
             pltpu.VMEM((RING, RING, 4, LANES), F32),
             pltpu.VMEM((RING, 1, LANES), F32),
             pltpu.VMEM((RING - 1, RING, 1, LANES), F32),
-            pltpu.VMEM((2 * TILE_W, PAIR * LANES), BF16),
-            pltpu.VMEM((TILE_W, PAIR * LANES), BF16),
+            pltpu.VMEM((2 * TILE_W, FOUR * LANES), BF16),
+            pltpu.VMEM((TILE_W, FOUR * LANES), BF16),
             pltpu.SemaphoreType.DMA((len(arrays),)),
             pltpu.SemaphoreType.DMA((stage_count,)),
             pltpu.SemaphoreType.DMA((stage_count, RING)),
@@ -408,6 +411,15 @@
         ),
         name="cluster_step",
     )(*arrays)
+    anywhere = pl.BlockSpec(memory_space=pl.ANY)
+    return pl.pallas_call(
+        store,
+        out_shape=outputs,
+        in_specs=[anywhere] * 2,
+        out_specs=(anywhere, anywhere),
+        scratch_shapes=[pltpu.SemaphoreType.DMA((2,))],
+        name="store",
+    )(*results)
 
 
 def solution(mesh):

time: 52.7 us -> 53.9 us (1.023)
  Pallas kernels: 49 us -> 53.1 us
  local copies, waits for them, and re-layouts: 2.86 us -> 0 us
    pallas_call x0 -> x1, Pallas kernels: none -> 5.28 us  [shards(): pl.pallas_call(store, out_shape=outputs, in_specs=[anywhere] * 2, out_spe...]
    unnamed x2 -> x0, local copies, waits for them, and re-layouts: 2.86 us -> none
    pallas_call x1, Pallas kernels: 49 us -> 47.8 us  [shards(): pl.pallas_call(functools.partial(kernel, 1.0 / stars, float(stars) ** (-2...]
where the time goes in v4:
time: 53.9 us; the launch traced here: 53.7 us
  Pallas kernels  53.1 us (99%)
  between operations  0.64 us (1%)
    pallas_call x1, Pallas kernels, shards(): pl.pallas_call(functools.partial(kernel, 1.0 / stars, float(stars) ** (-2...  47.8 us
    pallas_call x1, Pallas kernels, shards(): pl.pallas_call(store, out_shape=outputs, in_specs=[anywhere] * 2, out_spe...  5.28 us

profile of v4, /device:TPU:1, one launch (start us, length us, event | category | flops | bytes accessed | tf_op | source)
XLA Modules:
  0.0 53.7 jit_solution(7173750067173892137)
XLA Ops:
  0.6 47.8 %cluster_step.1 = (f32[12,16]{1,0:T(8,128)}, f32[2,1,128,128]{3,2,1,0:T(8,128)}) custom-call(f32[3,512]{1,0:T(4,128)} %pos_in.1, f32[3,512]{1,0:T(4,128)} %vel_in.1, f32[512]{0:T(512)} %mass_in.1, f32[6,16]{1,0:T(8,128)} %old_in.1, s32[16]{0:T(128)} %index_in.1, s32[16]{0:T(128)} %level_in.1, s32[16]{0:T(128)} %tile_in.1, s32[2,16]{1,0:T(2,128)} %offset_in.1), custom_call_target="tpu_custom_call" | custom-call | tf_op jit(solution)/shard_map/cluster_step/pallas_call | solution.py:377
  48.4 5.3 %store.1 = (f32[12,16]{1,0:T(8,128)}, f32[2,1,128,128]{3,2,1,0:T(8,128)}) custom-call(f32[12,16]{1,0:T(8,128)} %get-tuple-element.4.state_in, f32[2,1,128,128]{3,2,1,0:T(8,128)} %get-tuple-element.5.image_in), custom_call_target="tpu_custom_call" | custom-call | tf_op jit(solution)/shard_map/store/pallas_call | solution.py:415

commit v5 on v4

--- a/solution.py
+++ b/solution.py
@@ -355,17 +355,6 @@
         await_sent(7 + g, gathered.at[pl.ds(1, RING - 1), pl.ds(g * FOUR, FOUR)])
 
 
-def store(state_in, image_in, state_out, image_out, sem):
-    copies = [
-        pltpu.make_async_copy(state_in, state_out, sem.at[0]),
-        pltpu.make_async_copy(image_in, image_out, sem.at[1]),
-    ]
-    for one in reversed(copies):
-        one.start()
-    for one in copies:
-        one.wait()
-
-
 def shards(*arrays):
     stars = SRC * RING**3
     stage_count = 13
@@ -374,7 +363,7 @@
         jax.ShapeDtypeStruct((12, ACT), F32),
         jax.ShapeDtypeStruct((2, 1, TILE_W, TILE_W), F32),
     )
-    results = pl.pallas_call(
+    return pl.pallas_call(
         functools.partial(kernel, 1.0 / stars, float(stars) ** (-2.0 / 3.0)),
         out_shape=outputs,
         in_specs=[pl.BlockSpec(memory_space=pl.ANY)] * len(arrays),
@@ -407,19 +396,10 @@
             pltpu.SemaphoreType.DMA((stage_count, RING)),
         ],
         compiler_params=pltpu.CompilerParams(
-            collective_id=0, has_side_effects=True, vmem_limit_bytes=60 << 20
+            collective_id=0, has_side_effects=True, vmem_limit_bytes=48 << 20
         ),
         name="cluster_step",
-    )(*arrays)
-    anywhere = pl.BlockSpec(memory_space=pl.ANY)
-    return pl.pallas_call(
-        store,
-        out_shape=outputs,
-        in_specs=[anywhere] * 2,
-        out_specs=(anywhere, anywhere),
-        scratch_shapes=[pltpu.SemaphoreType.DMA((2,))],
-        name="store",
-    )(*results)
+    )(*[pltpu.with_memory_space_constraint(v, pltpu.HBM) for v in arrays])
 
 
 def solution(mesh):

time: 53.9 us -> 49.2 us (0.913)
  Pallas kernels: 53.1 us -> 47.1 us
  local copies, waits for them, and re-layouts: 0 us -> 1.26 us
    pallas_call x1 -> x0, Pallas kernels: 5.28 us -> none  [shards(): pl.pallas_call(store, out_shape=outputs, in_specs=[anywhere] * 2, out_spe...]
    unnamed x0 -> x2, local copies, waits for them, and re-layouts: none -> 1.26 us
    pallas_call x1, Pallas kernels: 47.8 us -> 47.1 us  [shards(): pl.pallas_call(functools.partial(kernel, 1.0 / stars, float(stars) ** (-2...]
where the time goes in v5:
time: 49.2 us; the launch traced here: 49 us
  Pallas kernels  47.1 us (96%)
  local copies, waits for them, and re-layouts  1.26 us (3%)
  between operations  0.64 us (1%)
    pallas_call x1, Pallas kernels, shards(): pl.pallas_call(functools.partial(kernel, 1.0 / stars, float(stars) ** (-2...  47.1 us
    unnamed x2, local copies, waits for them, and re-layouts  1.26 us

profile of v5, /device:TPU:1, one launch (start us, length us, event | category | flops | bytes accessed | tf_op | source)
XLA Modules:
  0.0 49.0 jit_solution(17377961771140078130)
XLA Ops:
  0.6 47.1 %cluster_step.1 = (f32[12,16]{1,0:T(8,128)S(1)}, f32[2,1,128,128]{3,2,1,0:T(8,128)S(1)}) custom-call(f32[3,512]{1,0:T(4,128)} %pos_in.1, f32[3,512]{1,0:T(4,128)} %vel_in.1, f32[512]{0:T(512)} %mass_in.1, f32[6,16]{1,0:T(8,128)} %old_in.1, s32[16]{0:T(128)} %index_in.1, s32[16]{0:T(128)} %level_in.1, s32[16]{0:T(128)} %tile_in.1, s32[2,16]{1,0:T(2,128)} %offset_in.1), custom_call_target="tpu_custom_call" | custom-call | tf_op jit(solution)/shard_map/cluster_step/pallas_call | solution.py:366
  47.8 0.6 %copy.12 = f32[12,16]{1,0:T(8,128)} copy(f32[12,16]{1,0:T(8,128)S(1)} %get-tuple-element.4) | data formatting | bytes 1536
  48.4 0.7 %copy.13 = f32[2,1,128,128]{3,2,1,0:T(8,128)} copy(f32[2,1,128,128]{3,2,1,0:T(8,128)S(1)} %get-tuple-element.5) | data formatting | bytes 262144

commit v6 on v5

--- a/solution.py
+++ b/solution.py
@@ -84,7 +84,7 @@
     state_ref, image_ref,
     pos_ref, vel_ref, mass_ref, old_ref, index_ref, level_ref, tile_ref, offset_ref,
     source, small, own, own_in, rest, rest_in, settled, targets, source_f, moments, near_f, dots_f,
-    part, part_in, half, half_in, spread, gathered, tiles, tiles_all, left, right,
+    part, part_in, spread, gathered, tiles, tiles_all, left, right,
     load_sem, send_sem, recv_sem,
 ):
     team, loop = lax.axis_index("team"), lax.axis_index("loop")
@@ -244,6 +244,15 @@
     def await_targets(s):
         copy(3, s, targets.at[0], targets.at[s], y_peer(s)).wait_recv()
 
+    def give(s, first):
+        back = (y + 8 - step_of(s)) % 8
+        for q in (4, 5, 2, 3, 6, 7, 1, 0):
+            if q >= first:
+                peer = at(back, z, (x + q // 2) % 4, (c + q % 2) % 2)
+                copy(4, 0, part.at[s], part_in.at[s * RING + q], peer).start()
+
+    give(0, 1)
+
     def force_step(i, carry):
         @pl.when(i == 0)
         def _():
@@ -270,29 +279,20 @@
 
         s = jnp.where(i < 2, 2 * i + 1, jnp.where(i == 2, 7, jnp.where(i == 3, 5, 14 - 2 * i)))
         combine(s, *force_sums(s, 0, RING))
-        copy(4, s, part.at[s], part_in.at[s], y_peer(s, -1)).start()
+        give(s, 0)
         return carry
 
     lax.fori_loop(0, RING - 1, force_step, 0)
 
-    total = part[0]
-    for s in (1, 3, 7, 5, 6, 4, 2):
-        copy(4, s, part.at[s], part_in.at[s], y_peer(s, -1)).wait_recv()
-        total = total + part_in[s]
-    half[...] = total
-    for s in (4, 5, 2, 3, 6, 7, 1):
-        copy(5, 0, half, half_in.at[s - 1], x_peer(s)).start()
     await_sent(0, own_in)
     await_sent(1, rest_in)
     await_sent(2, source.at[pl.ds(1, RING - 1)])
     await_sent(3, targets.at[pl.ds(1, RING - 1)])
-    await_sent(4, part.at[pl.ds(1, RING - 1)])
     await_sent(11, tiles.at[pl.ds(1, RING - 1)])
     await_sent(12, tiles_all)
     await_all(12, tiles_all)
-    await_all(5, half_in)
-    for s in slots:
-        total = total + half_in[s - 1]
+    await_all(4, part_in.at[pl.ds(1, RING * RING - 1)])
+    total = part[0] + jnp.sum(part_in[1:], axis=0)
 
     stars = targets[0]
     others = settled[...]
@@ -316,14 +316,16 @@
         scaled = cell - centre * reach
         return jnp.exp2(-(scaled * scaled))
 
-    def add_stars(blocks):
+    def build(half, blocks):
         for b, (rows, tile) in enumerate(blocks):
             here = tile == mine
             rows_y, rows_x = kernel_of(rows[2:3]), kernel_of(rows[3:4])
-            lanes = slice(b * LANES, (b + 1) * LANES)
+            lanes = slice((half * FOUR + b) * LANES, (half * FOUR + b + 1) * LANES)
             left[0:TILE_W, lanes] = (jnp.where(here, rows[0:1], 0.0) * rows_y).astype(BF16)
             left[TILE_W:, lanes] = (jnp.where(here, rows[1:2], 0.0) * rows_y).astype(BF16)
             right[:, lanes] = rows_x.astype(BF16)
+
+    def add_stars():
         out = lax.dot_general(
             left[...], right[...], (((1,), (1,)), ((), ())), preferred_element_type=F32
         )
@@ -334,22 +336,26 @@
             copy(6, s, spread.at[0], spread.at[s], z_peer(s)).wait_recv()
         for s in reversed(slots):
             four(g, s, y_peer(s)).start()
-        add_stars([(spread[g * FOUR + k], tiles[g * FOUR + k]) for k in range(FOUR)])
+        build(g, [(spread[g * FOUR + k], tiles[g * FOUR + k]) for k in range(FOUR)])
 
     shifted = pltpu.roll(pad_rows(state, 16), (LANES - place * ACT) % LANES, 1)
     state_ref[...] = shifted[0:12, 0:ACT]
     forward(0)
     forward(1)
-
-    def deposit_step(i, carry):
-        g = jnp.where((i < 6) | (i == 8), 0, 1)
-        s = jnp.where(i < 6, i + 1, jnp.where(i < 8, i - 5, jnp.where(i == 8, 7, i - 6)))
-        four(g, s, y_peer(s)).wait_recv()
-        add_stars([(gathered[s, g * FOUR + k], tiles_all[s - 1, g * FOUR + k]) for k in range(FOUR)])
+    add_stars()
+
+    def deposit_step(j, carry):
+        for half in (0, 1):
+            i = 2 * j + half
+            g = jnp.where((i < 6) | (i == 8), 0, 1)
+            s = jnp.where(i < 6, i + 1, jnp.where(i < 8, i - 5, jnp.where(i == 8, 7, i - 6)))
+            four(g, s, y_peer(s)).wait_recv()
+            build(half, [(gathered[s, g * FOUR + k], tiles_all[s - 1, g * FOUR + k]) for k in range(FOUR)])
+        add_stars()
         return carry
 
-    lax.fori_loop(0, 2 * (RING - 1), deposit_step, 0)
-    await_sent(5, half_in)
+    lax.fori_loop(0, RING - 1, deposit_step, 0)
+    await_sent(4, part_in.at[pl.ds(1, RING * RING - 1)])
     await_sent(6, spread.at[pl.ds(1, RING - 1)])
     for g in range(RING // FOUR):
         await_sent(7 + g, gathered.at[pl.ds(1, RING - 1), pl.ds(g * FOUR, FOUR)])
@@ -382,15 +388,13 @@
             pltpu.VMEM((LANES, RING * LANES), BF16),
             pltpu.VMEM((LANES, RING * LANES), BF16),
             pltpu.VMEM((RING, 8, LANES), F32),
-            pltpu.VMEM((RING, 8, LANES), F32),
-            pltpu.VMEM((8, LANES), F32),
-            pltpu.VMEM((RING - 1, 8, LANES), F32),
+            pltpu.VMEM((RING * RING, 8, LANES), F32),
             pltpu.VMEM((RING, 4, LANES), F32),
             pltpu.VMEM((RING, RING, 4, LANES), F32),
             pltpu.VMEM((RING, 1, LANES), F32),
             pltpu.VMEM((RING - 1, RING, 1, LANES), F32),
-            pltpu.VMEM((2 * TILE_W, FOUR * LANES), BF16),
-            pltpu.VMEM((TILE_W, FOUR * LANES), BF16),
+            pltpu.VMEM((2 * TILE_W, 2 * FOUR * LANES), BF16),
+            pltpu.VMEM((TILE_W, 2 * FOUR * LANES), BF16),
             pltpu.SemaphoreType.DMA((len(arrays),)),
             pltpu.SemaphoreType.DMA((stage_count,)),
             pltpu.SemaphoreType.DMA((stage_count, RING)),

time: 49.2 us -> 47.1 us (0.957)
  Pallas kernels: 47.1 us -> 45.1 us
    pallas_call x1, Pallas kernels: 47.1 us -> 45.1 us  [shards(): pl.pallas_call(functools.partial(kernel, 1.0 / stars, float(stars) ** (-2...]
where the time goes in v6:
time: 47.1 us; the launch traced here: 47 us
  Pallas kernels  45.1 us (96%)
  local copies, waits for them, and re-layouts  1.26 us (3%)
  between operations  0.64 us (1%)
    pallas_call x1, Pallas kernels, shards(): pl.pallas_call(functools.partial(kernel, 1.0 / stars, float(stars) ** (-2...  45.1 us
    unnamed x2, local copies, waits for them, and re-layouts  1.26 us

profile of v6, /device:TPU:1, one launch (start us, length us, event | category | flops | bytes accessed | tf_op | source)
XLA Modules:
  0.0 47.0 jit_solution(4572822508969991064)
XLA Ops:
  0.6 45.1 %cluster_step.1 = (f32[12,16]{1,0:T(8,128)S(1)}, f32[2,1,128,128]{3,2,1,0:T(8,128)S(1)}) custom-call(f32[3,512]{1,0:T(4,128)} %pos_in.1, f32[3,512]{1,0:T(4,128)} %vel_in.1, f32[512]{0:T(512)} %mass_in.1, f32[6,16]{1,0:T(8,128)} %old_in.1, s32[16]{0:T(128)} %index_in.1, s32[16]{0:T(128)} %level_in.1, s32[16]{0:T(128)} %tile_in.1, s32[2,16]{1,0:T(2,128)} %offset_in.1), custom_call_target="tpu_custom_call" | custom-call | tf_op jit(solution)/shard_map/cluster_step/pallas_call | solution.py:372
  45.7 0.6 %copy.12 = f32[12,16]{1,0:T(8,128)} copy(f32[12,16]{1,0:T(8,128)S(1)} %get-tuple-element.4) | data formatting | bytes 1536
  46.3 0.7 %copy.13 = f32[2,1,128,128]{3,2,1,0:T(8,128)} copy(f32[2,1,128,128]{3,2,1,0:T(8,128)S(1)} %get-tuple-element.5) | data formatting | bytes 262144

commit v7 on v6

--- a/solution.py
+++ b/solution.py
@@ -75,6 +75,9 @@
     return jnp.concatenate([pos, vel, force], axis=0)
 
 FOUR = 4
+ORDER = sorted(
+    ((a, b) for a in range(RING) for b in range(RING)), key=lambda p: ((p[0] + 1) // 2 + (p[1] + 1) // 2, p)
+)
 EARLY = 5
 
 
@@ -84,8 +87,8 @@
     state_ref, image_ref,
     pos_ref, vel_ref, mass_ref, old_ref, index_ref, level_ref, tile_ref, offset_ref,
     source, small, own, own_in, rest, rest_in, settled, targets, source_f, moments, near_f, dots_f,
-    part, part_in, spread, gathered, tiles, tiles_all, left, right,
-    load_sem, send_sem, recv_sem,
+    part, part_in, spread, gathered, tiles, tiles_in, tiles_all, left, right,
+    load_sem, send_sem, recv_sem, deposit_sem,
 ):
     team, loop = lax.axis_index("team"), lax.axis_index("loop")
     zh, y, c = team // 16, (team // 2) % 8, team % 2
@@ -165,10 +168,10 @@
 
     pl.semaphore_wait(barrier, 3 * (RING - 1))
 
+    for s in reversed(slots):
+        copy(2, s, source.at[0], source.at[s], z_peer(s)).start()
     for s in (4, 5, 2, 3, 6, 7, 1):
         copy(0, 0, own, own_in.at[s - 1], x_peer(s)).start()
-    for s in reversed(slots):
-        copy(2, s, source.at[0], source.at[s], z_peer(s)).start()
     for s in slots:
         copy(1, 0, rest, rest_in.at[s - 1], x_peer(s)).start()
 
@@ -275,7 +278,7 @@
         def _():
             await_all(11, tiles.at[pl.ds(1, RING - 1)])
             for s in slots:
-                copy(12, 0, tiles, tiles_all.at[s - 1], y_peer(s)).start()
+                copy(12, 0, tiles, tiles_in.at[s - 1], y_peer(s)).start()
 
         s = jnp.where(i < 2, 2 * i + 1, jnp.where(i == 2, 7, jnp.where(i == 3, 5, 14 - 2 * i)))
         combine(s, *force_sums(s, 0, RING))
@@ -289,8 +292,10 @@
     await_sent(2, source.at[pl.ds(1, RING - 1)])
     await_sent(3, targets.at[pl.ds(1, RING - 1)])
     await_sent(11, tiles.at[pl.ds(1, RING - 1)])
-    await_sent(12, tiles_all)
-    await_all(12, tiles_all)
+    await_sent(12, tiles_in)
+    await_all(12, tiles_in)
+    for i, (away_y, away_z) in enumerate(ORDER):
+        tiles_all[i] = tiles_in[away_y - 1, away_z] if away_y else tiles[away_z]
     await_all(4, part_in.at[pl.ds(1, RING * RING - 1)])
     total = part[0] + jnp.sum(part_in[1:], axis=0)
 
@@ -300,13 +305,33 @@
     centre_y = others[8:9] + (TILE_W / 16.0) * jnp.tanh(state[1:2])
     centre_x = others[9:10] + (TILE_W / 16.0) * jnp.tanh(state[0:1])
     mass = stars[6:7]
-    spread[0] = jnp.concatenate([mass, mass * state[5:6] * state[5:6], centre_y, centre_x], axis=0)
-    for s in reversed(slots):
-        copy(6, s, spread.at[0], spread.at[s], z_peer(s)).start()
-
-    def four(g, s, peer):
-        piece = pl.ds(g * FOUR, FOUR)
-        return copy(7 + g, s, spread.at[piece], gathered.at[s, piece], peer)
+    spread[...] = jnp.concatenate([mass, mass * state[5:6] * state[5:6], centre_y, centre_x], axis=0)
+    gathered[0] = spread[...]
+
+    def deposit(i):
+        away_y, away_z = ORDER[i]
+        return pltpu.make_async_remote_copy(
+            src_ref=spread,
+            dst_ref=gathered.at[i],
+            send_sem=send_sem.at[6],
+            recv_sem=deposit_sem.at[i // FOUR],
+            device_id=at((y + step_of(away_y)) % 8, (z + step_of(away_z)) % 8, x, c),
+            device_id_type=MESH,
+        )
+
+    for i in range(1, len(ORDER)):
+        deposit(i).start()
+
+    def await_deposits(first, count):
+        these = gathered.at[pl.ds(first, count)]
+        pltpu.make_async_remote_copy(
+            src_ref=these,
+            dst_ref=these,
+            send_sem=send_sem.at[6],
+            recv_sem=deposit_sem.at[first // FOUR],
+            device_id=y_peer(1),
+            device_id_type=MESH,
+        ).wait_recv()
 
     mine = (team * 8 + loop).astype(F32)
     reach = (40.0 / TILE_W) * math.sqrt(0.5 * math.log2(math.e))
@@ -331,34 +356,29 @@
         )
         image_ref[...] += out.reshape(2, 1, TILE_W, TILE_W)
 
-    def forward(g):
-        for s in range(max(1, g * FOUR), (g + 1) * FOUR):
-            copy(6, s, spread.at[0], spread.at[s], z_peer(s)).wait_recv()
-        for s in reversed(slots):
-            four(g, s, y_peer(s)).start()
-        build(g, [(spread[g * FOUR + k], tiles[g * FOUR + k]) for k in range(FOUR)])
-
     shifted = pltpu.roll(pad_rows(state, 16), (LANES - place * ACT) % LANES, 1)
     state_ref[...] = shifted[0:12, 0:ACT]
-    forward(0)
-    forward(1)
+
+    def build_four(half, first):
+        build(half, [(gathered[first + k], tiles_all[first + k]) for k in range(FOUR)])
+
+    await_deposits(1, FOUR - 1)
+    build_four(0, 0)
+    await_deposits(FOUR, FOUR)
+    build_four(1, FOUR)
     add_stars()
 
     def deposit_step(j, carry):
         for half in (0, 1):
-            i = 2 * j + half
-            g = jnp.where((i < 6) | (i == 8), 0, 1)
-            s = jnp.where(i < 6, i + 1, jnp.where(i < 8, i - 5, jnp.where(i == 8, 7, i - 6)))
-            four(g, s, y_peer(s)).wait_recv()
-            build(half, [(gathered[s, g * FOUR + k], tiles_all[s - 1, g * FOUR + k]) for k in range(FOUR)])
+            first = (2 * j + half) * FOUR
+            await_deposits(first, FOUR)
+            build_four(half, first)
         add_stars()
         return carry
 
-    lax.fori_loop(0, RING - 1, deposit_step, 0)
+    lax.fori_loop(1, RING, deposit_step, 0)
     await_sent(4, part_in.at[pl.ds(1, RING * RING - 1)])
-    await_sent(6, spread.at[pl.ds(1, RING - 1)])
-    for g in range(RING // FOUR):
-        await_sent(7 + g, gathered.at[pl.ds(1, RING - 1), pl.ds(g * FOUR, FOUR)])
+    await_sent(6, gathered.at[pl.ds(1, len(ORDER) - 1)])
 
 
 def shards(*arrays):
@@ -389,15 +409,17 @@
             pltpu.VMEM((LANES, RING * LANES), BF16),
             pltpu.VMEM((RING, 8, LANES), F32),
             pltpu.VMEM((RING * RING, 8, LANES), F32),
-            pltpu.VMEM((RING, 4, LANES), F32),
-            pltpu.VMEM((RING, RING, 4, LANES), F32),
+            pltpu.VMEM((4, LANES), F32),
+            pltpu.VMEM((RING * RING, 4, LANES), F32),
             pltpu.VMEM((RING, 1, LANES), F32),
             pltpu.VMEM((RING - 1, RING, 1, LANES), F32),
+            pltpu.VMEM((RING * RING, 1, LANES), F32),
             pltpu.VMEM((2 * TILE_W, 2 * FOUR * LANES), BF16),
             pltpu.VMEM((TILE_W, 2 * FOUR * LANES), BF16),
             pltpu.SemaphoreType.DMA((len(arrays),)),
             pltpu.SemaphoreType.DMA((stage_count,)),
             pltpu.SemaphoreType.DMA((stage_count, RING)),
+            pltpu.SemaphoreType.DMA((RING * RING // FOUR,)),
         ],
         compiler_params=pltpu.CompilerParams(
             collective_id=0, has_side_effects=True, vmem_limit_bytes=48 << 20

time: 47.1 us -> 47.3 us (level)
  no operation moved by 1% of the time
where the time goes in v7:
time: 47.3 us; the launch traced here: 47.1 us
  Pallas kernels  45.2 us (96%)
  local copies, waits for them, and re-layouts  1.26 us (3%)
  between operations  0.64 us (1%)
    pallas_call x1, Pallas kernels, shards(): pl.pallas_call(functools.partial(kernel, 1.0 / stars, float(stars) ** (-2...  45.2 us
    unnamed x2, local copies, waits for them, and re-layouts  1.26 us

profile of v7, /device:TPU:1, one launch (start us, length us, event | category | flops | bytes accessed | tf_op | source)
XLA Modules:
  0.0 47.1 jit_solution(9098965128354894563)
XLA Ops:
  0.6 45.2 %cluster_step.1 = (f32[12,16]{1,0:T(8,128)S(1)}, f32[2,1,128,128]{3,2,1,0:T(8,128)S(1)}) custom-call(f32[3,512]{1,0:T(4,128)} %pos_in.1, f32[3,512]{1,0:T(4,128)} %vel_in.1, f32[512]{0:T(512)} %mass_in.1, f32[6,16]{1,0:T(8,128)} %old_in.1, s32[16]{0:T(128)} %index_in.1, s32[16]{0:T(128)} %level_in.1, s32[16]{0:T(128)} %tile_in.1, s32[2,16]{1,0:T(2,128)} %offset_in.1), custom_call_target="tpu_custom_call" | custom-call | tf_op jit(solution)/shard_map/cluster_step/pallas_call | solution.py:392
  45.9 0.6 %copy.12 = f32[12,16]{1,0:T(8,128)} copy(f32[12,16]{1,0:T(8,128)S(1)} %get-tuple-element.4) | data formatting | bytes 1536
  46.5 0.7 %copy.13 = f32[2,1,128,128]{3,2,1,0:T(8,128)} copy(f32[2,1,128,128]{3,2,1,0:T(8,128)S(1)} %get-tuple-element.5) | data formatting | bytes 262144

commit v8 on v7

--- a/solution.py
+++ b/solution.py
@@ -238,14 +238,17 @@
         copy(11, 0, tiles.at[0], tiles.at[s], z_peer(s)).start()
     image_ref[...] = jnp.zeros_like(image_ref)
 
+    def await_targets(s):
+        copy(3, s, targets.at[0], targets.at[s], y_peer(s)).wait_recv()
+
+    await_targets(1)
+    prepare_targets(1, 2)
+    next_plain, next_tilted = force_sums(1, 0, EARLY)
     for s in range(EARLY, RING):
         await_source(s)
         prepare_source(s)
     more = force_sums(0, EARLY, RING)
     combine(0, plain + more[0], tilted + more[1])
-
-    def await_targets(s):
-        copy(3, s, targets.at[0], targets.at[s], y_peer(s)).wait_recv()
 
     def give(s, first):
         back = (y + 8 - step_of(s)) % 8
@@ -254,14 +257,10 @@
                 peer = at(back, z, (x + q // 2) % 4, (c + q % 2) % 2)
                 copy(4, 0, part.at[s], part_in.at[s * RING + q], peer).start()
 
-    give(0, 1)
+    def slot_of(i):
+        return jnp.where(i < 2, 2 * i + 1, jnp.where(i == 2, 7, jnp.where(i == 3, 5, 14 - 2 * i)))
 
     def force_step(i, carry):
-        @pl.when(i == 0)
-        def _():
-            await_targets(1)
-            prepare_targets(1, 2)
-
         @pl.when(i == 1)
         def _():
             await_targets(3)
@@ -280,12 +279,16 @@
             for s in slots:
                 copy(12, 0, tiles, tiles_in.at[s - 1], y_peer(s)).start()
 
-        s = jnp.where(i < 2, 2 * i + 1, jnp.where(i == 2, 7, jnp.where(i == 3, 5, 14 - 2 * i)))
+        s = slot_of(i)
+        give(slot_of(i - 1), 0)
         combine(s, *force_sums(s, 0, RING))
-        give(s, 0)
         return carry
 
-    lax.fori_loop(0, RING - 1, force_step, 0)
+    give(0, 1)
+    more = force_sums(1, EARLY, RING)
+    combine(1, next_plain + more[0], next_tilted + more[1])
+    lax.fori_loop(1, RING - 1, force_step, 0)
+    give(2, 0)
 
     await_sent(0, own_in)
     await_sent(1, rest_in)

time: 47.3 us -> 47.3 us (level)
  no operation moved by 1% of the time
where the time goes in v8:
time: 47.3 us; the launch traced here: 47.2 us
  Pallas kernels  45.3 us (96%)
  local copies, waits for them, and re-layouts  1.26 us (3%)
  between operations  0.64 us (1%)
    pallas_call x1, Pallas kernels, shards(): pl.pallas_call(functools.partial(kernel, 1.0 / stars, float(stars) ** (-2...  45.3 us
    unnamed x2, local copies, waits for them, and re-layouts  1.26 us

profile of v8, /device:TPU:1, one launch (start us, length us, event | category | flops | bytes accessed | tf_op | source)
XLA Modules:
  0.0 47.2 jit_solution(15265474820661346008)
XLA Ops:
  0.6 45.3 %cluster_step.1 = (f32[12,16]{1,0:T(8,128)S(1)}, f32[2,1,128,128]{3,2,1,0:T(8,128)S(1)}) custom-call(f32[3,512]{1,0:T(4,128)} %pos_in.1, f32[3,512]{1,0:T(4,128)} %vel_in.1, f32[512]{0:T(512)} %mass_in.1, f32[6,16]{1,0:T(8,128)} %old_in.1, s32[16]{0:T(128)} %index_in.1, s32[16]{0:T(128)} %level_in.1, s32[16]{0:T(128)} %tile_in.1, s32[2,16]{1,0:T(2,128)} %offset_in.1), custom_call_target="tpu_custom_call" | custom-call | tf_op jit(solution)/shard_map/cluster_step/pallas_call | solution.py:395
  45.9 0.6 %copy.12 = f32[12,16]{1,0:T(8,128)} copy(f32[12,16]{1,0:T(8,128)S(1)} %get-tuple-element.4) | data formatting | bytes 1536
  46.5 0.7 %copy.13 = f32[2,1,128,128]{3,2,1,0:T(8,128)} copy(f32[2,1,128,128]{3,2,1,0:T(8,128)S(1)} %get-tuple-element.5) | data formatting | bytes 262144

commit v9 on v8

--- a/solution.py
+++ b/solution.py
@@ -247,8 +247,6 @@
     for s in range(EARLY, RING):
         await_source(s)
         prepare_source(s)
-    more = force_sums(0, EARLY, RING)
-    combine(0, plain + more[0], tilted + more[1])
 
     def give(s, first):
         back = (y + 8 - step_of(s)) % 8
@@ -284,11 +282,13 @@
         combine(s, *force_sums(s, 0, RING))
         return carry
 
-    give(0, 1)
     more = force_sums(1, EARLY, RING)
     combine(1, next_plain + more[0], next_tilted + more[1])
     lax.fori_loop(1, RING - 1, force_step, 0)
     give(2, 0)
+    more = force_sums(0, EARLY, RING)
+    combine(0, plain + more[0], tilted + more[1])
+    give(0, 1)
 
     await_sent(0, own_in)
     await_sent(1, rest_in)

time: 47.3 us -> 46.6 us (0.985)
  Pallas kernels: 45.3 us -> 44.5 us
    pallas_call x1, Pallas kernels: 45.3 us -> 44.5 us  [shards(): pl.pallas_call(functools.partial(kernel, 1.0 / stars, float(stars) ** (-2...]
where the time goes in v9:
time: 46.6 us; the launch traced here: 46.4 us
  Pallas kernels  44.5 us (95%)
  local copies, waits for them, and re-layouts  1.26 us (3%)
  between operations  0.64 us (1%)
    pallas_call x1, Pallas kernels, shards(): pl.pallas_call(functools.partial(kernel, 1.0 / stars, float(stars) ** (-2...  44.5 us
    unnamed x2, local copies, waits for them, and re-layouts  1.26 us

profile of v9, /device:TPU:1, one launch (start us, length us, event | category | flops | bytes accessed | tf_op | source)
XLA Modules:
  0.0 46.4 jit_solution(13879981585685188079)
XLA Ops:
  0.6 44.5 %cluster_step.1 = (f32[12,16]{1,0:T(8,128)S(1)}, f32[2,1,128,128]{3,2,1,0:T(8,128)S(1)}) custom-call(f32[3,512]{1,0:T(4,128)} %pos_in.1, f32[3,512]{1,0:T(4,128)} %vel_in.1, f32[512]{0:T(512)} %mass_in.1, f32[6,16]{1,0:T(8,128)} %old_in.1, s32[16]{0:T(128)} %index_in.1, s32[16]{0:T(128)} %level_in.1, s32[16]{0:T(128)} %tile_in.1, s32[2,16]{1,0:T(2,128)} %offset_in.1), custom_call_target="tpu_custom_call" | custom-call | tf_op jit(solution)/shard_map/cluster_step/pallas_call | solution.py:395
  45.2 0.6 %copy.12 = f32[12,16]{1,0:T(8,128)} copy(f32[12,16]{1,0:T(8,128)S(1)} %get-tuple-element.4) | data formatting | bytes 1536
  45.8 0.7 %copy.13 = f32[2,1,128,128]{3,2,1,0:T(8,128)} copy(f32[2,1,128,128]{3,2,1,0:T(8,128)S(1)} %get-tuple-element.5) | data formatting | bytes 262144
